TPU v7x, 32 devices: a whole 2x2x4 slice. The times are simulated.
32 devices in a mesh: ka: 4 (over y, x), ea: 8 (over z, core).
Axes of the slice: x: 2, y: 2, z: 4, core: 2. Of those that a mesh axis runs over, the one named last changes fastest.
Arguments:
- lesser_in: float32 [4, 8, 2, 2, 128, 128], P('ka', 'ea'), may hold values from -6 to 6
- greater_in: float32 [4, 8, 2, 2, 128, 128], P('ka', 'ea'), may hold values from -6 to 6
- h_diag: float32 [4, 2, 2, 128, 128], P('ka'), may hold values from -0.035 to 0.45, as said below
- coupling: float32 [4, 1, 2, 128, 128], P('ka'), may hold values from -0.024 to 0.024
- contact: float32 [4, 8, 2, 2, 128, 128], P('ka', 'ea'), may hold values from -0.6 to 0.6
- coulomb: float32 [2, 128, 128], replicated, may hold values from 0.5 to 1.5
- tiles: int32 [16], replicated, may hold values from 0 to 31, as said below
Outputs:
- lesser_out: float32 [4, 8, 2, 2, 128, 128], P('ka', 'ea')
- greater_out: float32 [4, 8, 2, 2, 128, 128], P('ka', 'ea')
Inputs may be any that keep to these rules, and one draw needn't show every extreme that they name: The first 8 entries are the diagonal tiles 16 * b + 5 * r (r = 0 to 3) of each block b in order; then 4 distinct pairs, each an off-diagonal tile 16 * b + 4 * r + c with r < c followed by its transpose 16 * b + 4 * c + r. `h_diag`: every block is Hermitian: its real part is symmetric and its imaginary part antisymmetric.
All inputs are finite; a program needn't handle non-finite values.
Results may differ from a plain program's by a relative error of at most 0.0001.
Values sent between devices are 32-bit elements; how exact they have to be, the bound alone decides.
A program may use at most 128 MiB of HBM per device.

v0:
```python
import math
from functools import partial

import jax
import jax.numpy as jnp
import numpy as np
from jax import lax
from jax.experimental import pallas as pl
from jax.experimental.pallas import tpu as pltpu
from jax.sharding import PartitionSpec as P

BROADEN = 0.3
SPREAD = 0.05
SIGMA_SCALE = 0.01
PRECISE = lax.Precision.HIGHEST


def tiles_of(blocks):
    leading = blocks.shape[:-3]
    lead_rank = len(leading)
    block_count = blocks.shape[-3]
    tile_order = blocks.shape[-1] // 4
    viewed = blocks.reshape(leading + (block_count, 4, tile_order, 4, tile_order))
    viewed = jnp.moveaxis(viewed, lead_rank + 3, lead_rank + 2)
    return viewed.reshape(leading + (block_count * 16, tile_order, tile_order))


def blocks_of(pieces, block_count):
    leading = pieces.shape[:-3]
    lead_rank = len(leading)
    tile_order = pieces.shape[-1]
    viewed = pieces.reshape(leading + (block_count, 4, 4, tile_order, tile_order))
    viewed = jnp.moveaxis(viewed, lead_rank + 2, lead_rank + 3)
    return viewed.reshape(leading + (block_count, 4 * tile_order, 4 * tile_order))


def diag_order(tile_order):
    listing = [row_pos * tile_order + row_pos for row_pos in range(tile_order)]
    for row_pos in range(tile_order):
        for col_pos in range(row_pos + 1, tile_order):
            listing.append(row_pos * tile_order + col_pos)
            listing.append(col_pos * tile_order + row_pos)
    forward = np.array(listing, np.int32)
    return (forward, np.argsort(forward).astype(np.int32))


def arrange(pieces, diag_count):
    leading = pieces.shape[:-3]
    tile_order = pieces.shape[-1]
    forward = diag_order(tile_order)[0]
    diagonal = pieces[..., :diag_count, :, :].reshape(
        leading + (diag_count, tile_order * tile_order)
    )
    diagonal = jnp.take(diagonal, forward, axis=-1).reshape(leading + (-1,))
    paired = pieces[..., diag_count:, :, :].reshape(leading + (-1, 2, tile_order, tile_order))
    paired = jnp.stack([paired[..., 0, :, :], jnp.swapaxes(paired[..., 1, :, :], -1, -2)], axis=-1)
    return jnp.concatenate([diagonal, paired.reshape(leading + (-1,))], axis=-1)


def unarrange(flattened, diag_count, tile_order):
    leading = flattened.shape[:-1]
    square = tile_order * tile_order
    inverse = diag_order(tile_order)[1]
    diagonal = flattened[..., : diag_count * square].reshape(leading + (diag_count, square))
    diagonal = jnp.take(diagonal, inverse, axis=-1).reshape(
        leading + (diag_count, tile_order, tile_order)
    )
    paired = flattened[..., diag_count * square :].reshape(
        leading + (-1, tile_order, tile_order, 2)
    )
    paired = jnp.stack([paired[..., 0], jnp.swapaxes(paired[..., 1], -1, -2)], axis=-3)
    paired = paired.reshape(leading + (-1, tile_order, tile_order))
    return jnp.concatenate([diagonal, paired], axis=-3)


def partner(flattened, diag_count, tile_order):
    size_last = flattened.shape[-1]
    square = tile_order * tile_order
    flipped = flattened.reshape(flattened.shape[:-1] + (size_last // 2, 2))[..., ::-1].reshape(
        flattened.shape
    )
    position = jnp.arange(size_last, dtype=jnp.int32)
    itself = (position < diag_count * square) & (position % square < tile_order)
    return jnp.where(itself, flattened, flipped)


def tables(rows_count, cols_count, length):
    phases = (
        jnp.arange(rows_count, dtype=jnp.int32)[:, None]
        * jnp.arange(cols_count, dtype=jnp.int32)[None, :]
        % length
    )
    angles = phases.astype(jnp.float32) * (2.0 * math.pi / length)
    return (jnp.cos(angles), jnp.sin(angles))


def apply_table(coeffs, values):
    return jnp.einsum("fe,keal->kfal", coeffs, values, precision=PRECISE)


def transform(series, cosine, sine, sign, factor):
    real_in = series[..., 0, :]
    imag_in = series[..., 1, :]
    real_out = apply_table(cosine, real_in) + sign * apply_table(sine, imag_in)
    imag_out = apply_table(cosine, imag_in) - sign * apply_table(sine, real_in)
    return jnp.stack([real_out, imag_out], axis=-2) * factor


def pair_prod(first, second):
    first_re = first[..., 0, :]
    first_im = first[..., 1, :]
    second_re = second[..., 0, :]
    second_im = second[..., 1, :]
    return jnp.stack(
        [first_re * second_re - first_im * second_im, first_re * second_im + first_im * second_re],
        axis=-2,
    )


def pair_mul(first, second):
    products = jnp.einsum("bsij,btjk->bstik", first, second, precision=PRECISE)
    return jnp.stack(
        [products[:, 0, 0] - products[:, 1, 1], products[:, 0, 1] + products[:, 1, 0]], axis=1
    )


def dagger(matrix):
    swapped = jnp.swapaxes(matrix, -1, -2)
    return jnp.stack([swapped[:, 0], -swapped[:, 1]], axis=1)


def newton(system, twice_eye):
    real_d = jnp.diagonal(system[:, 0], axis1=-2, axis2=-1)
    imag_d = jnp.diagonal(system[:, 1], axis1=-2, axis2=-1)
    denominator = real_d * real_d + imag_d * imag_d
    inverse_re = real_d / denominator
    inverse_im = -imag_d / denominator
    scaled_re = system[:, 0] * inverse_re[:, None, :] - system[:, 1] * inverse_im[:, None, :]
    scaled_im = system[:, 0] * inverse_im[:, None, :] + system[:, 1] * inverse_re[:, None, :]
    inner_re = twice_eye[:, 0] - scaled_re
    inner_im = -scaled_im
    approx = jnp.stack(
        [
            inverse_re[:, :, None] * inner_re - inverse_im[:, :, None] * inner_im,
            inverse_re[:, :, None] * inner_im + inverse_im[:, :, None] * inner_re,
        ],
        axis=1,
    )
    approx = pair_mul(approx, twice_eye - pair_mul(system, approx))
    return approx


def polar_terms(direct, mirrored, scale_p):
    reflected = jnp.concatenate([mirrored[:, :1], jnp.flip(mirrored[:, 1:], axis=1)], axis=1)
    correlated = pair_prod(direct, reflected[:, :, ::-1])
    return jnp.stack([correlated[..., 1, :], -correlated[..., 0, :]], axis=-2) * scale_p


def self_energy(direct, screened, out_cos, out_sin, length, scale_p):
    convolved = transform(pair_prod(direct, screened), out_cos, out_sin, -1.0, 1.0 / length)
    return jnp.stack([-convolved[..., 1, :], convolved[..., 0, :]], axis=-2) * (
        SIGMA_SCALE * scale_p
    )


def on_device(lesser_in, greater_in, h_diag, coupling, contact, coulomb, tiles):
    k_local = lesser_in.shape[0]
    e_local = lesser_in.shape[1]
    block_count = lesser_in.shape[2]
    order_n = lesser_in.shape[-1]
    tile_order = order_n // 4
    diag_count = 4 * block_count
    devices_e = lax.axis_size("ea")
    devices_k = lax.axis_size("ka")
    e_total = e_local * devices_e
    length = 2 * e_total
    ret_local = tiles.shape[0] * tile_order * tile_order // devices_e
    offset = lax.axis_index("ea") * ret_local
    k_total = k_local * devices_k
    scale_p = 1.0 / math.sqrt(e_total)

    def layout(blocks):
        return arrange(jnp.take(tiles_of(jnp.moveaxis(blocks, 3, 2)), tiles, axis=-3), diag_count)

    greens = jnp.stack([layout(lesser_in), layout(greater_in)], axis=2)
    fwd_cos, fwd_sin = tables(length, e_total, length)
    full_cos, full_sin = tables(length, length, length)
    out_cos, out_sin = tables(e_total, length, length)
    coulomb_flat = arrange(jnp.take(tiles_of(coulomb), tiles, axis=-3), diag_count)
    outgoing = jnp.concatenate([greens, partner(greens, diag_count, tile_order)], axis=2)
    spectra = transform(
        lax.all_to_all(outgoing, "ea", split_axis=4, concat_axis=1, tiled=True),
        fwd_cos,
        fwd_sin,
        1.0,
        1.0,
    )
    direct = spectra[:, :, :2]
    mirrored = spectra[:, :, 2:]
    turned = polar_terms(direct, mirrored, scale_p)
    weight = lax.dynamic_slice_in_dim(coulomb_flat, offset, ret_local) ** 2
    lags = transform(jnp.sum(turned, axis=0, keepdims=True), full_cos, full_sin, -1.0, 1.0 / length)
    summed = lax.psum(lags, "ka")
    screened = transform(summed * (weight / k_total), full_cos, full_sin, 1.0, 1.0)
    sigma = self_energy(direct, screened, out_cos, out_sin, length, scale_p)
    returned = lax.all_to_all(sigma, "ea", split_axis=1, concat_axis=4, tiled=True)
    pieces = unarrange(returned, diag_count, tile_order)
    empty = jnp.zeros(pieces.shape[:-3] + (block_count * 16, tile_order, tile_order), jnp.float32)
    sigma_blocks = blocks_of(empty.at[..., tiles, :, :].set(pieces), block_count)
    sigma_ret = 0.5 * (sigma_blocks[:, :, 1] - sigma_blocks[:, :, 0])
    sigma_less = sigma_blocks[:, :, 0]
    batch = k_local * e_local
    identity = jnp.eye(order_n, dtype=jnp.float32)
    energy_idx = lax.axis_index("ea") * e_local + jnp.arange(e_local, dtype=jnp.int32)
    energies = -SPREAD + 2.0 * SPREAD * (energy_idx.astype(jnp.float32) + 0.5) / e_total
    energies = energies[None, :].reshape(batch)
    shifted = jnp.stack(
        [
            energies[:, None, None] * identity,
            jnp.broadcast_to(BROADEN * identity, (batch, order_n, order_n)),
        ],
        axis=1,
    )
    twice_eye = jnp.broadcast_to(
        jnp.stack([2.0 * identity, 0.0 * identity]), (batch, 2, order_n, order_n)
    )

    def per_energy(array_k):
        return array_k[:, None].reshape((batch,) + array_k.shape[1:])

    forward_r = []
    forward_l = []
    for blk_no in range(block_count):
        system = (
            shifted
            - per_energy(h_diag[:, blk_no])
            - sigma_ret[:, :, :, blk_no].reshape(batch, 2, order_n, order_n)
        )
        source = sigma_less[:, :, :, blk_no].reshape(batch, 2, order_n, order_n)
        if blk_no == 0:
            source = source + contact[:, :, 0].reshape(batch, 2, order_n, order_n)
        if blk_no == block_count - 1:
            source = source + contact[:, :, 1].reshape(batch, 2, order_n, order_n)
        if blk_no > 0:
            link = per_energy(coupling[:, blk_no - 1])
            system = system - pair_mul(dagger(link), pair_mul(forward_r[-1], link))
            source = source + pair_mul(dagger(link), pair_mul(forward_l[-1], link))
        green_r = newton(system, twice_eye)
        forward_r.append(green_r)
        forward_l.append(pair_mul(pair_mul(green_r, source), dagger(green_r)))
    retarded_list = [forward_r[-1]]
    lesser_list = [forward_l[-1]]
    blk_no = 0
    green_r = forward_r[blk_no]
    green_l = forward_l[blk_no]
    link = per_energy(coupling[:, blk_no])
    right_op = pair_mul(green_r, link)
    middle = pair_mul(right_op, retarded_list[0])
    new_r = green_r + pair_mul(middle, pair_mul(dagger(link), green_r))
    cross = pair_mul(middle, pair_mul(dagger(link), green_l))
    new_l = (
        green_l
        + pair_mul(pair_mul(right_op, lesser_list[0]), dagger(right_op))
        - cross
        - dagger(cross)
    )
    retarded_list.insert(0, new_r)
    lesser_list.insert(0, new_l)
    lesser = jnp.stack(lesser_list, axis=1)
    greater = jnp.stack(
        [
            lesser_list[blk_no] + retarded_list[blk_no] - dagger(retarded_list[blk_no])
            for blk_no in range(block_count)
        ],
        axis=1,
    )
    out_shape = (k_local, e_local, block_count, 2, order_n, order_n)
    return (lesser.reshape(out_shape), greater.reshape(out_shape))


MESH = pl.DeviceIdType.MESH
VMEM = pl.BlockSpec(memory_space=pltpu.VMEM)
SMEM = pl.BlockSpec(memory_space=pltpu.SMEM)


def half_swap(rows):
    return pltpu.roll(rows, 4, rows.ndim - 2)


def upper_half(shape):
    return lax.broadcasted_iota(jnp.int32, shape, len(shape) - 2) % 8 < 4


def tile_place(tiles_ref, slot):
    tile = tiles_ref[slot]
    return tile // 16, tile % 16 // 4, tile % 4


def pack_tiles(tiles_ref, load):
    group = lax.broadcasted_iota(jnp.int32, (32, 128), 1) // 32
    parts = []
    for blk in range(2):
        part = load(blk, 0)
        for pos in range(1, 4):
            part = jnp.where(group == pos, load(blk, 32 * pos), part)
        parts.append(part)
    for half in range(2):
        part = None
        for pos in range(4):
            blk, row, col = tile_place(tiles_ref, 8 + 4 * half + pos)
            slab = load(blk, pl.multiple_of(32 * row, 32))
            slab = pltpu.roll(slab, (pos + 4 - col) % 4 * 32, 1)
            part = slab if part is None else jnp.where(group == pos, slab, part)
        parts.append(part)
    return jnp.concatenate(parts, axis=0).reshape(16, 8, 128)


def pack_kernel(tiles_ref, l_ref, g_ref, c_ref, out_ref, weight_ref, gt_ref, ct_ref):
    top = upper_half((16, 8, 128))
    for blk in range(2):
        ct_ref[blk] = c_ref[blk].T
        for part in range(2):
            gt_ref[blk, part] = g_ref[blk, part].T
    for kind, ref in ((0, l_ref), (1, gt_ref)):
        real = pack_tiles(tiles_ref, lambda blk, row: ref[blk, 0, pl.ds(row, 32), :])
        imag = pack_tiles(tiles_ref, lambda blk, row: ref[blk, 1, pl.ds(row, 32), :])
        out_ref[:, 0, kind] = jnp.where(top, real, half_swap(imag))
        out_ref[:, 1, kind] = jnp.where(top, half_swap(real), imag)
    for kind, ref in ((0, c_ref), (1, ct_ref)):
        bare = pack_tiles(tiles_ref, lambda blk, row: ref[blk, pl.ds(row, 32), :])
        bare = bare * bare
        weight_ref[:, 0, kind] = jnp.where(top, bare, half_swap(bare))
        weight_ref[:, 1, kind] = jnp.where(top, half_swap(bare), bare)


def exchange_kernel(
    n_k, n_e, send_ref, weight_ref, out_ref, held, sigma, back, send_a, recv_a, send_b, recv_b
):
    count = n_k * n_e
    me = lax.axis_index("ka") * n_e + lax.axis_index("ea")

    def place(other):
        return {"ka": other // n_e, "ea": other % n_e}

    def forward(other):
        return pltpu.make_async_remote_copy(
            src_ref=send_ref.at[other],
            dst_ref=held.at[me],
            send_sem=send_a.at[other],
            recv_sem=recv_a.at[me],
            device_id=place(other),
            device_id_type=MESH,
        )

    def arrival(other):
        return pltpu.make_async_remote_copy(
            src_ref=send_ref.at[other],
            dst_ref=held.at[other],
            send_sem=send_a.at[other],
            recv_sem=recv_a.at[other],
            device_id=place(other),
            device_id_type=MESH,
        )

    def backward(other):
        return pltpu.make_async_remote_copy(
            src_ref=sigma.at[other],
            dst_ref=back.at[me],
            send_sem=send_b.at[other],
            recv_sem=recv_b.at[me],
            device_id=place(other),
            device_id_type=MESH,
        )

    def returned(other):
        return pltpu.make_async_remote_copy(
            src_ref=sigma.at[other],
            dst_ref=back.at[other],
            send_sem=send_b.at[other],
            recv_sem=recv_b.at[other],
            device_id=place(other),
            device_id_type=MESH,
        )

    def others(body):
        def step(index, carry):
            body((me + index) % count)
            return carry

        lax.fori_loop(1, count, step, 0)

    barrier = pltpu.get_barrier_semaphore()
    others(
        lambda other: pl.semaphore_signal(
            barrier, inc=1, device_id=place(other), device_id_type=MESH
        )
    )
    pl.semaphore_wait(barrier, count - 1)
    others(lambda other: forward(other).start())
    held[me] = send_ref[me]
    others(lambda other: arrival(other).wait_recv())

    lags = 2 * n_e - 1

    def correlate(k_index, sums):
        plain, crossed = list(sums[0]), list(sums[1])
        lesser = [held[k_index * n_e + e, 0] for e in range(n_e)]
        greater = [held[k_index * n_e + e, 1] for e in range(n_e)]
        for e_two in range(n_e):
            swapped = half_swap(greater[e_two])
            for e_one in range(n_e):
                lag = e_one - e_two + n_e - 1
                plain[lag] = plain[lag] + lesser[e_one] * greater[e_two]
                crossed[lag] = crossed[lag] + lesser[e_one] * swapped
        return tuple(plain), tuple(crossed)

    zero = jnp.zeros((8, 128), jnp.float32)
    plain, crossed = lax.fori_loop(0, n_k, correlate, ((zero,) * lags, (zero,) * lags))
    sign = jnp.where(upper_half((8, 128)), 1.0, -1.0)
    scale = SIGMA_SCALE / (n_e * n_k)
    weight_l = weight_ref[me, 0] * scale
    weight_g = weight_ref[me, 1] * scale
    real = [sign * (total - half_swap(total)) for total in plain]
    imag = [-sign * (total + half_swap(total)) for total in crossed]

    def convolve(k_index, carry):
        first = k_index * n_e
        for kind, weight in ((0, weight_l), (1, weight_g)):
            green = [held[first + e, kind] for e in range(n_e)]
            swapped = [half_swap(piece) for piece in green]
            for e_out in range(n_e):
                total = None
                for e_in in range(n_e):
                    lag = e_out - e_in if kind == 0 else e_in - e_out
                    lag = lag + n_e - 1
                    term = green[e_in] * real[lag] + swapped[e_in] * imag[lag]
                    total = term if total is None else total + term
                sigma[first + e_out, kind] = total * weight

        def send(e_out, inner):
            @pl.when(first + e_out != me)
            def _():
                backward(first + e_out).start()

            return inner

        lax.fori_loop(0, n_e, send, 0)
        return carry

    lax.fori_loop(0, n_k, convolve, 0)
    back[me] = sigma[me]
    others(lambda other: returned(other).wait_recv())
    out_ref[...] = back[...]
    others(lambda other: forward(other).wait_send())
    others(lambda other: backward(other).wait_send())


def split(value):
    high = value.astype(jnp.bfloat16)
    return high, (value - high.astype(jnp.float32)).astype(jnp.bfloat16)


def square_form(rows):
    real, imag = rows[:, :128], rows[:, 128:]
    return split(jnp.concatenate([rows, jnp.concatenate([-imag, real], axis=1)], axis=0))


def times(first, second, contract=0):
    dims = (((1,), (contract,)), ((), ()))

    def dot(left, right):
        return lax.dot_general(left, right, dims, preferred_element_type=jnp.float32)

    high, low = first
    return dot(high, second[0]) + (dot(high, second[1]) + dot(low, second[0]))


def adjoint(rows):
    return jnp.concatenate([rows[:, :128].T, -rows[:, 128:].T], axis=1)


def invert_rows(system, eye):
    real_m, imag_m = system[:, :128], system[:, 128:]
    only_re = jnp.where(eye, real_m, 0.0)
    only_im = jnp.where(eye, imag_m, 0.0)

    def reciprocal(axis):
        real_d = jnp.sum(only_re, axis=axis, keepdims=True)
        imag_d = jnp.sum(only_im, axis=axis, keepdims=True)
        denominator = real_d * real_d + imag_d * imag_d
        return real_d / denominator, -imag_d / denominator

    row_re, row_im = reciprocal(0)
    col_re, col_im = reciprocal(1)
    twice = jnp.where(eye, 2.0, 0.0)
    inner_re = twice - (real_m * row_re - imag_m * row_im)
    inner_im = -(real_m * row_im + imag_m * row_re)
    approx = jnp.concatenate(
        [col_re * inner_re - col_im * inner_im, col_re * inner_im + col_im * inner_re], axis=1
    )
    product = times(split(system), square_form(approx))
    rest = jnp.concatenate([twice - product[:, :128], -product[:, 128:]], axis=1)
    return times(split(approx), square_form(rest))


def sweep_kernel(
    tiles_ref, energy_ref, sigma_ref, h_ref, link_ref, contact_ref, lesser_ref, greater_ref, blocks
):
    top = upper_half((16, 8, 128))
    group = lax.broadcasted_iota(jnp.int32, (32, 128), 1) // 32
    for kind in range(2):
        first, second = sigma_ref[:, 0, kind], sigma_ref[:, 1, kind]
        parts = (
            jnp.where(top, first, half_swap(second)),
            jnp.where(top, half_swap(first), second),
        )
        for part in range(2):
            packed = parts[part].reshape(128, 128)
            for blk in range(2):
                for pos in range(4):
                    blocks[kind, part, blk, 32 * pos : 32 * pos + 32, :] = jnp.where(
                        group == pos, packed[32 * blk : 32 * blk + 32], 0.0
                    )
            for slot in range(8):
                blk, row, col = tile_place(tiles_ref, 8 + slot)
                start = 64 + 32 * (slot // 4)
                slab = pltpu.roll(packed[start : start + 32], (col + 4 - slot % 4) % 4 * 32, 1)
                rows = pl.ds(pl.multiple_of(32 * row, 32), 32)
                blocks[kind, part, blk, rows, :] = jnp.where(
                    group == col, slab, blocks[kind, part, blk, rows, :]
                )

    eye = lax.broadcasted_iota(jnp.int32, (128, 128), 0) == lax.broadcasted_iota(
        jnp.int32, (128, 128), 1
    )
    shift = jnp.concatenate(
        [jnp.where(eye, energy_ref[0], 0.0), jnp.where(eye, BROADEN, 0.0)], axis=1
    )

    def rows_of(ref, *index):
        return jnp.concatenate([ref[*index, 0], ref[*index, 1]], axis=1)

    def system_source(blk):
        less = jnp.concatenate([blocks[0, 0, blk], blocks[0, 1, blk]], axis=1)
        more = jnp.concatenate([blocks[1, 0, blk].T, blocks[1, 1, blk].T], axis=1)
        system = shift - rows_of(h_ref, blk) - 0.5 * (more - less)
        return system, less + rows_of(contact_ref, blk)

    link = rows_of(link_ref, 0)
    link_square = square_form(link)
    link_adjoint = split(adjoint(link))

    system_0, source_0 = system_source(0)
    system_1, source_1 = system_source(1)
    gr_0 = invert_rows(system_0, eye)
    gr_0_rows, gr_0_square = split(gr_0), square_form(gr_0)
    right_op = times(gr_0_rows, link_square)
    right_square = square_form(right_op)
    system_1 = system_1 - times(link_adjoint, right_square)
    gr_1 = invert_rows(system_1, eye)
    gl_0 = times(split(times(gr_0_rows, square_form(source_0))), gr_0_square, 1)
    left_l = times(link_adjoint, square_form(gl_0))
    source_1 = source_1 + times(split(left_l), link_square)
    gr_1_square = square_form(gr_1)
    gl_1 = times(split(times(split(gr_1), square_form(source_1))), gr_1_square, 1)
    left_r = times(link_adjoint, gr_0_square)
    right_rows = split(right_op)
    middle = split(times(right_rows, gr_1_square))
    full_r = gr_0 + times(middle, square_form(left_r))
    cross = times(middle, square_form(left_l))
    inner = times(split(times(right_rows, square_form(gl_1))), right_square, 1)
    full_l = gl_0 + inner - cross - adjoint(cross)
    for blk, retarded, lesser in ((0, full_r, full_l), (1, gr_1, gl_1)):
        greater = lesser + retarded - adjoint(retarded)
        for part in range(2):
            lesser_ref[blk, part] = lesser[:, 128 * part : 128 * part + 128]
            greater_ref[blk, part] = greater[:, 128 * part : 128 * part + 128]


def small_device(n_k, n_e, lesser_in, greater_in, h_diag, coupling, contact, coulomb, tiles):
    count = n_k * n_e
    f32 = jnp.float32
    limit = pltpu.CompilerParams(vmem_limit_bytes=32 * 1024 * 1024)
    packed, weight = pl.pallas_call(
        pack_kernel,
        out_shape=(jax.ShapeDtypeStruct((16, 2, 2, 8, 128), f32),) * 2,
        in_specs=[SMEM, VMEM, VMEM, VMEM],
        out_specs=(VMEM, VMEM),
        scratch_shapes=[pltpu.VMEM((2, 2, 128, 128), f32), pltpu.VMEM((2, 128, 128), f32)],
        compiler_params=limit,
        name="pack",
    )(tiles, lesser_in[0, 0], greater_in[0, 0], coulomb)
    slots = (count, 2, 8, 128)
    sigma = pl.pallas_call(
        partial(exchange_kernel, n_k, n_e),
        out_shape=jax.ShapeDtypeStruct(slots, f32),
        in_specs=[VMEM, VMEM],
        out_specs=VMEM,
        scratch_shapes=[pltpu.VMEM(slots, f32)] * 3 + [pltpu.SemaphoreType.DMA((count,))] * 4,
        compiler_params=pltpu.CompilerParams(
            collective_id=0, has_side_effects=True, vmem_limit_bytes=32 * 1024 * 1024
        ),
        name="exchange",
    )(packed.reshape(slots), weight.reshape(slots))
    energy = -SPREAD + 2.0 * SPREAD * (lax.axis_index("ea").astype(f32) + 0.5) / n_e
    lesser, greater = pl.pallas_call(
        sweep_kernel,
        out_shape=(jax.ShapeDtypeStruct((2, 2, 128, 128), f32),) * 2,
        in_specs=[SMEM, SMEM, VMEM, VMEM, VMEM, VMEM],
        out_specs=(VMEM, VMEM),
        scratch_shapes=[pltpu.VMEM((2, 2, 2, 128, 128), f32)],
        compiler_params=limit,
        name="sweep",
    )(
        tiles,
        energy.reshape(1),
        sigma.reshape(16, 2, 2, 8, 128),
        h_diag[0],
        coupling[0],
        contact[0, 0],
    )
    return lesser[None, None], greater[None, None]


def per_device(mesh, lesser_in, *rest):
    n_k, n_e = mesh.shape["ka"], mesh.shape["ea"]
    fits = n_k * n_e == 32 and lesser_in.shape == (1, 1, 2, 2, 128, 128) and rest[-1].shape == (16,)
    if fits:
        return small_device(n_k, n_e, lesser_in, *rest)
    return on_device(lesser_in, *rest)


def solution(mesh):
    in_specs = (
        P("ka", "ea", None, None, None, None),
        P("ka", "ea", None, None, None, None),
        P("ka", None, None, None, None),
        P("ka", None, None, None, None),
        P("ka", "ea", None, None, None, None),
        P(),
        P(),
    )
    out_specs = (P("ka", "ea", None, None, None, None), P("ka", "ea", None, None, None, None))
    return jax.shard_map(
        partial(per_device, mesh), mesh=mesh, in_specs=in_specs, out_specs=out_specs, check_vma=False
    )
```

profile of v0, /device:TPU:5, one launch (start us, length us, event | category | flops | bytes accessed | tf_op | source)
XLA Modules:
  0.0 33.8 jit_solution(6823577159182755676)
XLA Ops:
  0.6 0.0 copy-start.6
  0.6 0.6 %copy-done.6 = s32[16]{0:T(128)S(1)} copy-done((s32[16]{0:T(128)S(1)}, s32[16]{0:T(128)}, u32[]{:S(2)}) %copy-start.6) | copy-done | bytes 88
  1.3 0.0 copy-start
  1.3 0.9 %copy-done = f32[1,1,2,2,128,128]{5,4,3,2,1,0:T(8,128)S(1)} copy-done((f32[1,1,2,2,128,128]{5,4,3,2,1,0:T(8,128)S(1)}, f32[1,1,2,2,128,128]{5,4,3,2,1,0:T(8,128)}, u32[]{:S(2)}) %copy-start) | copy-done | bytes 262168
  2.2 0.0 copy-start.1
  2.2 0.9 %copy-done.1 = f32[1,1,2,2,128,128]{5,4,3,2,1,0:T(8,128)S(1)} copy-done((f32[1,1,2,2,128,128]{5,4,3,2,1,0:T(8,128)S(1)}, f32[1,1,2,2,128,128]{5,4,3,2,1,0:T(8,128)}, u32[]{:S(2)}) %copy-start.1) | copy-done | bytes 262168
  3.2 0.0 copy-start.4
  3.2 0.9 %copy-done.4 = f32[2,128,128]{2,1,0:T(8,128)S(1)} copy-done((f32[2,128,128]{2,1,0:T(8,128)S(1)}, f32[2,128,128]{2,1,0:T(8,128)}, u32[]{:S(2)}) %copy-start.4) | copy-done | bytes 131096
  4.1 1.1 %pack.1 = (f32[16,2,2,8,128]{4,3,2,1,0:T(8,128)S(1)}, f32[16,2,2,8,128]{4,3,2,1,0:T(8,128)S(1)}) custom-call(s32[16]{0:T(128)S(1)} %copy-done.6, f32[2,2,128,128]{3,2,1,0:T(8,128)S(1)} %bitcast.14, f32[2,2,128,128]{3,2,1,0:T(8,128)S(1)} %bitcast.15, f32[2,128,128]{2,1,0:T(8,128)S(1)} %copy-done.4), custom_call_target="tpu_custom_call" | custom-call | tf_op jit(solution)/shard_map/pack/pallas_call | solution.py:584
  5.2 0.0 copy-start.2
  5.2 0.0 copy-start.3
  5.2 0.0 copy-start.5
  5.2 23.3 %exchange.1 = f32[32,2,8,128]{3,2,1,0:T(8,128)S(1)} custom-call(f32[32,2,8,128]{3,2,1,0:T(8,128)S(1)} %bitcast.12, f32[32,2,8,128]{3,2,1,0:T(8,128)S(1)} %bitcast.13), custom_call_target="tpu_custom_call" | custom-call | tf_op jit(solution)/shard_map/exchange/pallas_call | solution.py:594
  28.5 0.0 copy-done.2
  28.6 0.0 copy-done.3
  28.6 0.0 copy-done.5
  28.6 5.2 %sweep.1 = (f32[2,2,128,128]{3,2,1,0:T(8,128)}, f32[2,2,128,128]{3,2,1,0:T(8,128)}) custom-call(s32[16]{0:T(128)S(1)} %copy-done.6, f32[1]{0:T(128)} %bitcast.energy_ref, f32[16,2,2,8,128]{4,3,2,1,0:T(8,128)S(1)} %bitcast.11, f32[2,2,128,128]{3,2,1,0:T(8,128)S(1)} %bitcast.16, f32[1,2,128,128]{3,2,1,0:T(8,128)S(1)} %bitcast.18, f32[2,2,128,128]{3,2,1,0:T(8,128)S(1)} %bitcast.17), custom_call_target="tpu_custom_call" | custom-call | tf_op jit(solution)/shard_map/sweep/pallas_call | solution.py:606
Async XLA Ops:
  0.6 0.7 %copy-start.6 = (s32[16]{0:T(128)S(1)}, s32[16]{0:T(128)}, u32[]{:S(2)}) copy-start(s32[16]{0:T(128)} %tiles_ref.3) | copy-start | bytes 196
  1.3 0.9 %copy-start = (f32[1,1,2,2,128,128]{5,4,3,2,1,0:T(8,128)S(1)}, f32[1,1,2,2,128,128]{5,4,3,2,1,0:T(8,128)}, u32[]{:S(2)}) copy-start(f32[1,1,2,2,128,128]{5,4,3,2,1,0:T(8,128)} %param.7) | copy-start | bytes 786436
  2.2 0.9 %copy-start.1 = (f32[1,1,2,2,128,128]{5,4,3,2,1,0:T(8,128)S(1)}, f32[1,1,2,2,128,128]{5,4,3,2,1,0:T(8,128)}, u32[]{:S(2)}) copy-start(f32[1,1,2,2,128,128]{5,4,3,2,1,0:T(8,128)} %param.8) | copy-start | bytes 786436
  3.2 0.9 %copy-start.4 = (f32[2,128,128]{2,1,0:T(8,128)S(1)}, f32[2,128,128]{2,1,0:T(8,128)}, u32[]{:S(2)}) copy-start(f32[2,128,128]{2,1,0:T(8,128)} %c_ref.1) | copy-start | bytes 393220
  5.2 23.4 %copy-start.2 = (f32[1,2,2,128,128]{4,3,2,1,0:T(8,128)S(1)}, f32[1,2,2,128,128]{4,3,2,1,0:T(8,128)}, u32[]{:S(2)}) copy-start(f32[1,2,2,128,128]{4,3,2,1,0:T(8,128)} %param.9) | copy-start | bytes 786436
  5.2 23.4 %copy-start.3 = (f32[1,1,2,2,128,128]{5,4,3,2,1,0:T(8,128)S(1)}, f32[1,1,2,2,128,128]{5,4,3,2,1,0:T(8,128)}, u32[]{:S(2)}) copy-start(f32[1,1,2,2,128,128]{5,4,3,2,1,0:T(8,128)} %param.11) | copy-start | bytes 786436
  5.2 23.4 %copy-start.5 = (f32[1,1,2,128,128]{4,3,2,1,0:T(8,128)S(1)}, f32[1,1,2,128,128]{4,3,2,1,0:T(8,128)}, u32[]{:S(2)}) copy-start(f32[1,1,2,128,128]{4,3,2,1,0:T(8,128)} %param.10) | copy-start | bytes 393220
where the time goes:
time: 34 us; the launch traced here: 33.8 us
  Pallas kernels  29.6 us (87%)
  local copies, waits for them, and re-layouts  3.47 us (10%)
  between operations  0.71 us (2%)
    pallas_call x1, Pallas kernels, small_device(): pl.pallas_call(partial(exchange_kernel, n_k, n_e), out_shape=jax.ShapeDty...  23.3 us
    pallas_call x1, Pallas kernels, small_device(): pl.pallas_call(sweep_kernel, out_shape=(jax.ShapeDtypeStruct((2, 2, 128,...  5.21 us
    unnamed x14, local copies, waits for them, and re-layouts  3.47 us
    pallas_call x1, Pallas kernels, small_device(): pl.pallas_call(pack_kernel, out_shape=(jax.ShapeDtypeStruct((16, 2, 2, 8,...  1.06 us

commit v1 on v0

--- a/solution.py
+++ b/solution.py
@@ -281,6 +281,7 @@
 MESH = pl.DeviceIdType.MESH
 VMEM = pl.BlockSpec(memory_space=pltpu.VMEM)
 SMEM = pl.BlockSpec(memory_space=pltpu.SMEM)
+HBM = pl.BlockSpec(memory_space=pltpu.HBM)
 
 
 def half_swap(rows):
@@ -298,114 +299,163 @@
 
 def pack_tiles(tiles_ref, load):
     group = lax.broadcasted_iota(jnp.int32, (32, 128), 1) // 32
+    slabs = [[load(blk, 32 * pos) for pos in range(4)] for blk in range(2)]
     parts = []
     for blk in range(2):
-        part = load(blk, 0)
+        part = slabs[blk][0]
         for pos in range(1, 4):
-            part = jnp.where(group == pos, load(blk, 32 * pos), part)
+            part = jnp.where(group == pos, slabs[blk][pos], part)
         parts.append(part)
     for half in range(2):
         part = None
         for pos in range(4):
             blk, row, col = tile_place(tiles_ref, 8 + 4 * half + pos)
-            slab = load(blk, pl.multiple_of(32 * row, 32))
-            slab = pltpu.roll(slab, (pos + 4 - col) % 4 * 32, 1)
+            slab = slabs[0][0]
+            for index in range(1, 8):
+                found = blk * 4 + row == index
+                slab = jnp.where(found, slabs[index // 4][index % 4], slab)
+            turn = (pos + 4 - col) % 4
+            slab = jnp.where(turn % 2 == 1, pltpu.roll(slab, 32, 1), slab)
+            slab = jnp.where(turn >= 2, pltpu.roll(slab, 64, 1), slab)
             part = slab if part is None else jnp.where(group == pos, slab, part)
         parts.append(part)
     return jnp.concatenate(parts, axis=0).reshape(16, 8, 128)
 
 
-def pack_kernel(tiles_ref, l_ref, g_ref, c_ref, out_ref, weight_ref, gt_ref, ct_ref):
+def exchange_kernel(
+    n_k,
+    n_e,
+    tiles_hbm,
+    l_hbm,
+    g_hbm,
+    c_hbm,
+    out_ref,
+    tiles_ref,
+    l_ref,
+    g_ref,
+    c_ref,
+    gt_ref,
+    ct_ref,
+    packed,
+    weight_ref,
+    held,
+    sigma,
+    back,
+    load_sem,
+    send_a,
+    recv_a,
+    send_b,
+    recv_b,
+):
+    count = n_k * n_e
+    half = n_e // 2
+    my_k = lax.axis_index("ka")
+    my_e = lax.axis_index("ea")
+    me = my_k * n_e + my_e
+    side = my_e // half
+
+    loads = [
+        pltpu.make_async_copy(source, target, load_sem.at[index])
+        for index, (source, target) in enumerate(
+            ((tiles_hbm, tiles_ref), (g_hbm, g_ref), (l_hbm, l_ref), (c_hbm, c_ref))
+        )
+    ]
+    for load in loads:
+        load.start()
+
+    def place(other):
+        return {"ka": other // n_e, "ea": other % n_e}
+
+    def remote(source, slot, send_sem, recv_sem, other):
+        return pltpu.make_async_remote_copy(
+            src_ref=source,
+            dst_ref=slot,
+            send_sem=send_sem,
+            recv_sem=recv_sem,
+            device_id=place(other),
+            device_id_type=MESH,
+        )
+
+    def forward(other):
+        source = packed.at[other // 2, other % 2]
+        return remote(source, held.at[me], send_a.at[other], recv_a.at[me], other)
+
+    def arrival(other):
+        source = packed.at[other // 2, other % 2]
+        return remote(source, held.at[other], send_a.at[other], recv_a.at[other], other)
+
+    def backward(other):
+        return remote(sigma.at[other], back.at[me], send_b.at[other], recv_b.at[me], other)
+
+    def returned(other):
+        return remote(sigma.at[other], back.at[other], send_b.at[other], recv_b.at[other], other)
+
+    def others(body):
+        def step(index, carry):
+            turn = (side + 1 + index // (n_k * half)) % 2
+            rest = index % (n_k * half)
+            energy = turn * half + (my_e + rest) % half
+            body((my_k + rest // half) % n_k * n_e + energy)
+            return carry
+
+        lax.fori_loop(0, n_k * half, step, 0)
+        lax.fori_loop(n_k * half + 1, count, step, 0)
+
+    barrier = pltpu.get_barrier_semaphore()
+    others(
+        lambda other: pl.semaphore_signal(
+            barrier, inc=1, device_id=place(other), device_id_type=MESH
+        )
+    )
+
     top = upper_half((16, 8, 128))
+
+    def pack(kind, ref):
+        real = pack_tiles(tiles_ref, lambda blk, row: ref[blk, 0, pl.ds(row, 32), :])
+        imag = pack_tiles(tiles_ref, lambda blk, row: ref[blk, 1, pl.ds(row, 32), :])
+        packed[:, 0, kind] = jnp.where(top, real, half_swap(imag))
+        packed[:, 1, kind] = jnp.where(top, half_swap(real), imag)
+
+    loads[0].wait()
+    loads[1].wait()
+    for blk in range(2):
+        for part in range(2):
+            gt_ref[blk, part] = g_ref[blk, part].T
+    pack(1, gt_ref)
+    loads[2].wait()
+    pack(0, l_ref)
+    pl.semaphore_wait(barrier, count - 1)
+    others(lambda other: forward(other).start())
+
+    held[me] = packed[me // 2, me % 2]
+    loads[3].wait()
     for blk in range(2):
         ct_ref[blk] = c_ref[blk].T
-        for part in range(2):
-            gt_ref[blk, part] = g_ref[blk, part].T
-    for kind, ref in ((0, l_ref), (1, gt_ref)):
-        real = pack_tiles(tiles_ref, lambda blk, row: ref[blk, 0, pl.ds(row, 32), :])
-        imag = pack_tiles(tiles_ref, lambda blk, row: ref[blk, 1, pl.ds(row, 32), :])
-        out_ref[:, 0, kind] = jnp.where(top, real, half_swap(imag))
-        out_ref[:, 1, kind] = jnp.where(top, half_swap(real), imag)
     for kind, ref in ((0, c_ref), (1, ct_ref)):
         bare = pack_tiles(tiles_ref, lambda blk, row: ref[blk, pl.ds(row, 32), :])
         bare = bare * bare
         weight_ref[:, 0, kind] = jnp.where(top, bare, half_swap(bare))
         weight_ref[:, 1, kind] = jnp.where(top, half_swap(bare), bare)
-
-
-def exchange_kernel(
-    n_k, n_e, send_ref, weight_ref, out_ref, held, sigma, back, send_a, recv_a, send_b, recv_b
-):
-    count = n_k * n_e
-    me = lax.axis_index("ka") * n_e + lax.axis_index("ea")
-
-    def place(other):
-        return {"ka": other // n_e, "ea": other % n_e}
-
-    def forward(other):
-        return pltpu.make_async_remote_copy(
-            src_ref=send_ref.at[other],
-            dst_ref=held.at[me],
-            send_sem=send_a.at[other],
-            recv_sem=recv_a.at[me],
-            device_id=place(other),
-            device_id_type=MESH,
-        )
-
-    def arrival(other):
-        return pltpu.make_async_remote_copy(
-            src_ref=send_ref.at[other],
-            dst_ref=held.at[other],
-            send_sem=send_a.at[other],
-            recv_sem=recv_a.at[other],
-            device_id=place(other),
-            device_id_type=MESH,
-        )
-
-    def backward(other):
-        return pltpu.make_async_remote_copy(
-            src_ref=sigma.at[other],
-            dst_ref=back.at[me],
-            send_sem=send_b.at[other],
-            recv_sem=recv_b.at[me],
-            device_id=place(other),
-            device_id_type=MESH,
-        )
-
-    def returned(other):
-        return pltpu.make_async_remote_copy(
-            src_ref=sigma.at[other],
-            dst_ref=back.at[other],
-            send_sem=send_b.at[other],
-            recv_sem=recv_b.at[other],
-            device_id=place(other),
-            device_id_type=MESH,
-        )
-
-    def others(body):
-        def step(index, carry):
-            body((me + index) % count)
+    scale = SIGMA_SCALE / (n_e * n_k)
+    weight_l = weight_ref[me // 2, me % 2, 0] * scale
+    weight_g = weight_ref[me // 2, me % 2, 1] * scale
+
+    lags = 2 * n_e - 1
+
+    def correlate(turn, sums):
+        first = (my_k + turn) % n_k * n_e
+
+        def arrive(e, carry):
+            @pl.when(first + e != me)
+            def _():
+                arrival(first + e).wait_recv()
+
             return carry
 
-        lax.fori_loop(1, count, step, 0)
-
-    barrier = pltpu.get_barrier_semaphore()
-    others(
-        lambda other: pl.semaphore_signal(
-            barrier, inc=1, device_id=place(other), device_id_type=MESH
-        )
-    )
-    pl.semaphore_wait(barrier, count - 1)
-    others(lambda other: forward(other).start())
-    held[me] = send_ref[me]
-    others(lambda other: arrival(other).wait_recv())
-
-    lags = 2 * n_e - 1
-
-    def correlate(k_index, sums):
+        lax.fori_loop(0, n_e, arrive, 0)
         plain, crossed = list(sums[0]), list(sums[1])
-        lesser = [held[k_index * n_e + e, 0] for e in range(n_e)]
-        greater = [held[k_index * n_e + e, 1] for e in range(n_e)]
+        lesser = [held[first + e, 0] for e in range(n_e)]
+        greater = [held[first + e, 1] for e in range(n_e)]
         for e_two in range(n_e):
             swapped = half_swap(greater[e_two])
             for e_one in range(n_e):
@@ -417,14 +467,11 @@
     zero = jnp.zeros((8, 128), jnp.float32)
     plain, crossed = lax.fori_loop(0, n_k, correlate, ((zero,) * lags, (zero,) * lags))
     sign = jnp.where(upper_half((8, 128)), 1.0, -1.0)
-    scale = SIGMA_SCALE / (n_e * n_k)
-    weight_l = weight_ref[me, 0] * scale
-    weight_g = weight_ref[me, 1] * scale
     real = [sign * (total - half_swap(total)) for total in plain]
     imag = [-sign * (total + half_swap(total)) for total in crossed]
 
-    def convolve(k_index, carry):
-        first = k_index * n_e
+    def convolve(turn, carry):
+        first = (my_k + turn) % n_k * n_e
         for kind, weight in ((0, weight_l), (1, weight_g)):
             green = [held[first + e, kind] for e in range(n_e)]
             swapped = [half_swap(piece) for piece in green]
@@ -437,10 +484,12 @@
                     total = term if total is None else total + term
                 sigma[first + e_out, kind] = total * weight
 
-        def send(e_out, inner):
-            @pl.when(first + e_out != me)
+        def send(index, inner):
+            other = first + (side + 1 + index // half) % 2 * half + (my_e + index) % half
+
+            @pl.when(other != me)
             def _():
-                backward(first + e_out).start()
+                backward(other).start()
 
             return inner
 
@@ -449,10 +498,10 @@
 
     lax.fori_loop(0, n_k, convolve, 0)
     back[me] = sigma[me]
+    others(lambda other: forward(other).wait_send())
+    others(lambda other: backward(other).wait_send())
     others(lambda other: returned(other).wait_recv())
     out_ref[...] = back[...]
-    others(lambda other: forward(other).wait_send())
-    others(lambda other: backward(other).wait_send())
 
 
 def split(value):
@@ -472,7 +521,8 @@
         return lax.dot_general(left, right, dims, preferred_element_type=jnp.float32)
 
     high, low = first
-    return dot(high, second[0]) + (dot(high, second[1]) + dot(low, second[0]))
+    both = dot(jnp.concatenate([high, low], axis=0), second[0])
+    return both[:128] + (dot(high, second[1]) + both[128:])
 
 
 def adjoint(rows):
@@ -504,10 +554,23 @@
 
 
 def sweep_kernel(
-    tiles_ref, energy_ref, sigma_ref, h_ref, link_ref, contact_ref, lesser_ref, greater_ref, blocks
+    tiles_hbm,
+    energy_ref,
+    sigma_ref,
+    h_ref,
+    link_ref,
+    contact_ref,
+    lesser_ref,
+    greater_ref,
+    blocks,
+    tiles_ref,
+    load_sem,
 ):
+    load = pltpu.make_async_copy(tiles_hbm, tiles_ref, load_sem)
+    load.start()
     top = upper_half((16, 8, 128))
     group = lax.broadcasted_iota(jnp.int32, (32, 128), 1) // 32
+    pieces = []
     for kind in range(2):
         first, second = sigma_ref[:, 0, kind], sigma_ref[:, 1, kind]
         parts = (
@@ -516,19 +579,22 @@
         )
         for part in range(2):
             packed = parts[part].reshape(128, 128)
+            pieces.append((kind, part, packed[64:]))
             for blk in range(2):
                 for pos in range(4):
                     blocks[kind, part, blk, 32 * pos : 32 * pos + 32, :] = jnp.where(
                         group == pos, packed[32 * blk : 32 * blk + 32], 0.0
                     )
-            for slot in range(8):
-                blk, row, col = tile_place(tiles_ref, 8 + slot)
-                start = 64 + 32 * (slot // 4)
-                slab = pltpu.roll(packed[start : start + 32], (col + 4 - slot % 4) % 4 * 32, 1)
-                rows = pl.ds(pl.multiple_of(32 * row, 32), 32)
-                blocks[kind, part, blk, rows, :] = jnp.where(
-                    group == col, slab, blocks[kind, part, blk, rows, :]
-                )
+    load.wait()
+    for slot in range(8):
+        blk, row, col = tile_place(tiles_ref, 8 + slot)
+        start = 32 * (slot // 4)
+        rows = pl.ds(pl.multiple_of(32 * row, 32), 32)
+        for kind, part, packed in pieces:
+            slab = pltpu.roll(packed[start : start + 32], (col + 4 - slot % 4) % 4 * 32, 1)
+            blocks[kind, part, blk, rows, :] = jnp.where(
+                group == col, slab, blocks[kind, part, blk, rows, :]
+            )
 
     eye = lax.broadcasted_iota(jnp.int32, (128, 128), 0) == lax.broadcasted_iota(
         jnp.int32, (128, 128), 1
@@ -577,42 +643,47 @@
             greater_ref[blk, part] = greater[:, 128 * part : 128 * part + 128]
 
 
+def in_hbm(array):
+    return pltpu.with_memory_space_constraint(array, pltpu.HBM)
+
+
 def small_device(n_k, n_e, lesser_in, greater_in, h_diag, coupling, contact, coulomb, tiles):
     count = n_k * n_e
     f32 = jnp.float32
     limit = pltpu.CompilerParams(vmem_limit_bytes=32 * 1024 * 1024)
-    packed, weight = pl.pallas_call(
-        pack_kernel,
-        out_shape=(jax.ShapeDtypeStruct((16, 2, 2, 8, 128), f32),) * 2,
-        in_specs=[SMEM, VMEM, VMEM, VMEM],
-        out_specs=(VMEM, VMEM),
-        scratch_shapes=[pltpu.VMEM((2, 2, 128, 128), f32), pltpu.VMEM((2, 128, 128), f32)],
-        compiler_params=limit,
-        name="pack",
-    )(tiles, lesser_in[0, 0], greater_in[0, 0], coulomb)
     slots = (count, 2, 8, 128)
+    blocks = pltpu.VMEM((2, 2, 128, 128), f32)
+    plane = pltpu.VMEM((2, 128, 128), f32)
     sigma = pl.pallas_call(
         partial(exchange_kernel, n_k, n_e),
         out_shape=jax.ShapeDtypeStruct(slots, f32),
-        in_specs=[VMEM, VMEM],
+        in_specs=[HBM] * 4,
         out_specs=VMEM,
-        scratch_shapes=[pltpu.VMEM(slots, f32)] * 3 + [pltpu.SemaphoreType.DMA((count,))] * 4,
+        scratch_shapes=[pltpu.SMEM((16,), jnp.int32), blocks, blocks, plane, blocks, plane]
+        + [pltpu.VMEM((16, 2, 2, 8, 128), f32)] * 2
+        + [pltpu.VMEM(slots, f32)] * 3
+        + [pltpu.SemaphoreType.DMA((4,))]
+        + [pltpu.SemaphoreType.DMA((count,))] * 4,
         compiler_params=pltpu.CompilerParams(
             collective_id=0, has_side_effects=True, vmem_limit_bytes=32 * 1024 * 1024
         ),
         name="exchange",
-    )(packed.reshape(slots), weight.reshape(slots))
+    )(*(in_hbm(array) for array in (tiles, lesser_in[0, 0], greater_in[0, 0], coulomb)))
     energy = -SPREAD + 2.0 * SPREAD * (lax.axis_index("ea").astype(f32) + 0.5) / n_e
     lesser, greater = pl.pallas_call(
         sweep_kernel,
         out_shape=(jax.ShapeDtypeStruct((2, 2, 128, 128), f32),) * 2,
-        in_specs=[SMEM, SMEM, VMEM, VMEM, VMEM, VMEM],
+        in_specs=[HBM, SMEM, VMEM, VMEM, VMEM, VMEM],
         out_specs=(VMEM, VMEM),
-        scratch_shapes=[pltpu.VMEM((2, 2, 2, 128, 128), f32)],
+        scratch_shapes=[
+            pltpu.VMEM((2, 2, 2, 128, 128), f32),
+            pltpu.SMEM((16,), jnp.int32),
+            pltpu.SemaphoreType.DMA,
+        ],
         compiler_params=limit,
         name="sweep",
     )(
-        tiles,
+        in_hbm(tiles),
         energy.reshape(1),
         sigma.reshape(16, 2, 2, 8, 128),
         h_diag[0],

time: 34 us -> 31.3 us (0.921)
  the two profiles are of different devices: /device:TPU:5 before, /device:TPU:0 now
where the time goes in v1:
time: 31.3 us; the launch traced here: 31.1 us
  Pallas kernels  30.4 us (97%)
  between operations  0.7 us (2%)
    pallas_call x1, Pallas kernels, small_device(): pl.pallas_call(partial(exchange_kernel, n_k, n_e), out_shape=jax.ShapeDty...  25.4 us
    pallas_call x1, Pallas kernels, small_device(): pl.pallas_call(sweep_kernel, out_shape=(jax.ShapeDtypeStruct((2, 2, 128,...  5.06 us

profile of v1, /device:TPU:0, one launch (start us, length us, event | category | flops | bytes accessed | tf_op | source)
XLA Modules:
  0.0 31.1 jit_solution(15157101863301050799)
XLA Ops:
  0.6 0.0 copy-start
  0.6 0.0 copy-start.1
  0.7 0.0 copy-start.2
  0.7 25.4 %exchange.1 = f32[32,2,8,128]{3,2,1,0:T(8,128)S(1)} custom-call(s32[16]{0:T(128)} %tiles_hbm.3, f32[2,2,128,128]{3,2,1,0:T(8,128)} %bitcast.13, f32[2,2,128,128]{3,2,1,0:T(8,128)} %bitcast.14, f32[2,128,128]{2,1,0:T(8,128)} %c_hbm.1), custom_call_target="tpu_custom_call" | custom-call | tf_op jit(solution)/shard_map/exchange/pallas_call | solution.py:657
  26.1 0.0 copy-done
  26.1 0.0 copy-done.1
  26.1 0.0 copy-done.2
  26.1 5.1 %sweep.1 = (f32[2,2,128,128]{3,2,1,0:T(8,128)}, f32[2,2,128,128]{3,2,1,0:T(8,128)}) custom-call(s32[16]{0:T(128)} %tiles_hbm.3, f32[1]{0:T(128)} %bitcast.energy_ref, f32[16,2,2,8,128]{4,3,2,1,0:T(8,128)S(1)} %bitcast.9, f32[2,2,128,128]{3,2,1,0:T(8,128)S(1)} %bitcast.10, f32[1,2,128,128]{3,2,1,0:T(8,128)S(1)} %bitcast.12, f32[2,2,128,128]{3,2,1,0:T(8,128)S(1)} %bitcast.11), custom_call_target="tpu_custom_call" | custom-call | tf_op jit(solution)/shard_map/sweep/pallas_call | solution.py:673
Async XLA Ops:
  0.6 25.4 %copy-start = (f32[1,2,2,128,128]{4,3,2,1,0:T(8,128)S(1)}, f32[1,2,2,128,128]{4,3,2,1,0:T(8,128)}, u32[]{:S(2)}) copy-start(f32[1,2,2,128,128]{4,3,2,1,0:T(8,128)} %param.9) | copy-start | bytes 786436
  0.6 25.4 %copy-start.1 = (f32[1,1,2,2,128,128]{5,4,3,2,1,0:T(8,128)S(1)}, f32[1,1,2,2,128,128]{5,4,3,2,1,0:T(8,128)}, u32[]{:S(2)}) copy-start(f32[1,1,2,2,128,128]{5,4,3,2,1,0:T(8,128)} %param.11) | copy-start | bytes 786436
  0.7 25.4 %copy-start.2 = (f32[1,1,2,128,128]{4,3,2,1,0:T(8,128)S(1)}, f32[1,1,2,128,128]{4,3,2,1,0:T(8,128)}, u32[]{:S(2)}) copy-start(f32[1,1,2,128,128]{4,3,2,1,0:T(8,128)} %param.10) | copy-start | bytes 393220

commit v2 on v1

--- a/solution.py
+++ b/solution.py
@@ -363,58 +363,37 @@
     for load in loads:
         load.start()
 
-    def place(other):
-        return {"ka": other // n_e, "ea": other % n_e}
-
-    def remote(source, slot, send_sem, recv_sem, other):
+    k_list = [(my_k + step) % n_k for step in range(n_k)]
+    near = [side * half + (my_e + step) % half for step in range(half)]
+    far = [(1 - side) * half + (my_e + step) % half for step in range(half)]
+    others = [(k, e) for k in k_list for e in far]
+    others += [(k, e) for k in k_list for e in near][1:]
+
+    def remote(source, target, send_sem, recv_sem, k, e):
         return pltpu.make_async_remote_copy(
             src_ref=source,
-            dst_ref=slot,
+            dst_ref=target,
             send_sem=send_sem,
             recv_sem=recv_sem,
-            device_id=place(other),
+            device_id={"ka": k, "ea": e},
             device_id_type=MESH,
         )
 
-    def forward(other):
-        source = packed.at[other // 2, other % 2]
-        return remote(source, held.at[me], send_a.at[other], recv_a.at[me], other)
-
-    def arrival(other):
-        source = packed.at[other // 2, other % 2]
-        return remote(source, held.at[other], send_a.at[other], recv_a.at[other], other)
-
-    def backward(other):
-        return remote(sigma.at[other], back.at[me], send_b.at[other], recv_b.at[me], other)
-
-    def returned(other):
-        return remote(sigma.at[other], back.at[other], send_b.at[other], recv_b.at[other], other)
-
-    def others(body):
-        def step(index, carry):
-            turn = (side + 1 + index // (n_k * half)) % 2
-            rest = index % (n_k * half)
-            energy = turn * half + (my_e + rest) % half
-            body((my_k + rest // half) % n_k * n_e + energy)
-            return carry
-
-        lax.fori_loop(0, n_k * half, step, 0)
-        lax.fori_loop(n_k * half + 1, count, step, 0)
+    def all_of(ref, send_sem, recv_sem):
+        every = ref.at[pl.ds(0, count - 1)]
+        return remote(every, every, send_sem, recv_sem, *others[0])
 
     barrier = pltpu.get_barrier_semaphore()
-    others(
-        lambda other: pl.semaphore_signal(
-            barrier, inc=1, device_id=place(other), device_id_type=MESH
-        )
-    )
+    for k, e in others:
+        pl.semaphore_signal(barrier, inc=1, device_id={"ka": k, "ea": e}, device_id_type=MESH)
 
     top = upper_half((16, 8, 128))
 
     def pack(kind, ref):
         real = pack_tiles(tiles_ref, lambda blk, row: ref[blk, 0, pl.ds(row, 32), :])
         imag = pack_tiles(tiles_ref, lambda blk, row: ref[blk, 1, pl.ds(row, 32), :])
-        packed[:, 0, kind] = jnp.where(top, real, half_swap(imag))
-        packed[:, 1, kind] = jnp.where(top, half_swap(real), imag)
+        packed[:16, kind] = jnp.where(top, real, half_swap(imag))
+        packed[16:, kind] = jnp.where(top, half_swap(real), imag)
 
     loads[0].wait()
     loads[1].wait()
@@ -425,34 +404,27 @@
     loads[2].wait()
     pack(0, l_ref)
     pl.semaphore_wait(barrier, count - 1)
-    others(lambda other: forward(other).start())
-
-    held[me] = packed[me // 2, me % 2]
+    for k, e in others:
+        other = k * n_e + e
+        remote(packed.at[other], held.at[me], send_a, recv_a, k, e).start()
+
+    held[me] = packed[me]
     loads[3].wait()
     for blk in range(2):
         ct_ref[blk] = c_ref[blk].T
     for kind, ref in ((0, c_ref), (1, ct_ref)):
         bare = pack_tiles(tiles_ref, lambda blk, row: ref[blk, pl.ds(row, 32), :])
         bare = bare * bare
-        weight_ref[:, 0, kind] = jnp.where(top, bare, half_swap(bare))
-        weight_ref[:, 1, kind] = jnp.where(top, half_swap(bare), bare)
+        weight_ref[:16, kind] = jnp.where(top, bare, half_swap(bare))
+        weight_ref[16:, kind] = jnp.where(top, half_swap(bare), bare)
     scale = SIGMA_SCALE / (n_e * n_k)
-    weight_l = weight_ref[me // 2, me % 2, 0] * scale
-    weight_g = weight_ref[me // 2, me % 2, 1] * scale
+    weight_l = weight_ref[me, 0] * scale
+    weight_g = weight_ref[me, 1] * scale
 
     lags = 2 * n_e - 1
 
-    def correlate(turn, sums):
-        first = (my_k + turn) % n_k * n_e
-
-        def arrive(e, carry):
-            @pl.when(first + e != me)
-            def _():
-                arrival(first + e).wait_recv()
-
-            return carry
-
-        lax.fori_loop(0, n_e, arrive, 0)
+    def correlate(k_index, sums):
+        first = k_index * n_e
         plain, crossed = list(sums[0]), list(sums[1])
         lesser = [held[first + e, 0] for e in range(n_e)]
         greater = [held[first + e, 1] for e in range(n_e)]
@@ -464,6 +436,7 @@
                 crossed[lag] = crossed[lag] + lesser[e_one] * swapped
         return tuple(plain), tuple(crossed)
 
+    all_of(held, send_a, recv_a).wait_recv()
     zero = jnp.zeros((8, 128), jnp.float32)
     plain, crossed = lax.fori_loop(0, n_k, correlate, ((zero,) * lags, (zero,) * lags))
     sign = jnp.where(upper_half((8, 128)), 1.0, -1.0)
@@ -471,7 +444,8 @@
     imag = [-sign * (total + half_swap(total)) for total in crossed]
 
     def convolve(turn, carry):
-        first = (my_k + turn) % n_k * n_e
+        k_index = (my_k + turn) % n_k
+        first = k_index * n_e
         for kind, weight in ((0, weight_l), (1, weight_g)):
             green = [held[first + e, kind] for e in range(n_e)]
             swapped = [half_swap(piece) for piece in green]
@@ -484,23 +458,24 @@
                     total = term if total is None else total + term
                 sigma[first + e_out, kind] = total * weight
 
-        def send(index, inner):
-            other = first + (side + 1 + index // half) % 2 * half + (my_e + index) % half
-
-            @pl.when(other != me)
-            def _():
-                backward(other).start()
-
-            return inner
-
-        lax.fori_loop(0, n_e, send, 0)
+        def send(e):
+            source = sigma.at[first + e]
+            remote(source, back.at[me], send_b, recv_b, k_index, e).start()
+
+        for e in far + near[1:]:
+            send(e)
+
+        @pl.when(turn > 0)
+        def _():
+            send(my_e)
+
         return carry
 
     lax.fori_loop(0, n_k, convolve, 0)
     back[me] = sigma[me]
-    others(lambda other: forward(other).wait_send())
-    others(lambda other: backward(other).wait_send())
-    others(lambda other: returned(other).wait_recv())
+    all_of(held, send_a, recv_a).wait_send()
+    all_of(back, send_b, recv_b).wait_send()
+    all_of(back, send_b, recv_b).wait_recv()
     out_ref[...] = back[...]
 
 
@@ -572,7 +547,7 @@
     group = lax.broadcasted_iota(jnp.int32, (32, 128), 1) // 32
     pieces = []
     for kind in range(2):
-        first, second = sigma_ref[:, 0, kind], sigma_ref[:, 1, kind]
+        first, second = sigma_ref[:16, kind], sigma_ref[16:, kind]
         parts = (
             jnp.where(top, first, half_swap(second)),
             jnp.where(top, half_swap(first), second),
@@ -660,10 +635,9 @@
         in_specs=[HBM] * 4,
         out_specs=VMEM,
         scratch_shapes=[pltpu.SMEM((16,), jnp.int32), blocks, blocks, plane, blocks, plane]
-        + [pltpu.VMEM((16, 2, 2, 8, 128), f32)] * 2
-        + [pltpu.VMEM(slots, f32)] * 3
+        + [pltpu.VMEM(slots, f32)] * 5
         + [pltpu.SemaphoreType.DMA((4,))]
-        + [pltpu.SemaphoreType.DMA((count,))] * 4,
+        + [pltpu.SemaphoreType.DMA] * 4,
         compiler_params=pltpu.CompilerParams(
             collective_id=0, has_side_effects=True, vmem_limit_bytes=32 * 1024 * 1024
         ),
@@ -685,7 +659,7 @@
     )(
         in_hbm(tiles),
         energy.reshape(1),
-        sigma.reshape(16, 2, 2, 8, 128),
+        sigma,
         h_diag[0],
         coupling[0],
         contact[0, 0],

time: 31.3 us -> 29.1 us (0.930)
  Pallas kernels: 30.4 us -> 28.3 us
    pallas_call x1, Pallas kernels: 25.4 us -> 23.2 us  [small_device(): pl.pallas_call(partial(exchange_kernel, n_k, n_e), out_shape=jax.ShapeDty...]
where the time goes in v2:
time: 29.1 us; the launch traced here: 29 us
  Pallas kernels  28.3 us (97%)
  between operations  0.7 us (2%)
    pallas_call x1, Pallas kernels, small_device(): pl.pallas_call(partial(exchange_kernel, n_k, n_e), out_shape=jax.ShapeDty...  23.2 us
    pallas_call x1, Pallas kernels, small_device(): pl.pallas_call(sweep_kernel, out_shape=(jax.ShapeDtypeStruct((2, 2, 128,...  5.06 us

profile of v2, /device:TPU:0, one launch (start us, length us, event | category | flops | bytes accessed | tf_op | source)
XLA Modules:
  0.0 29.0 jit_solution(4913204949543013502)
XLA Ops:
  0.6 0.0 copy-start
  0.6 0.0 copy-start.1
  0.7 0.0 copy-start.2
  0.7 23.2 %exchange.1.sigma_ref = f32[32,2,8,128]{3,2,1,0:T(8,128)S(1)} custom-call(s32[16]{0:T(128)} %tiles_hbm.3, f32[2,2,128,128]{3,2,1,0:T(8,128)} %bitcast.11, f32[2,2,128,128]{3,2,1,0:T(8,128)} %bitcast.12, f32[2,128,128]{2,1,0:T(8,128)} %c_hbm.1), custom_call_target="tpu_custom_call" | custom-call | tf_op jit(solution)/shard_map/exchange/pallas_call | solution.py:632
  23.9 0.0 copy-done
  23.9 0.0 copy-done.1
  23.9 0.0 copy-done.2
  23.9 5.1 %sweep.1 = (f32[2,2,128,128]{3,2,1,0:T(8,128)}, f32[2,2,128,128]{3,2,1,0:T(8,128)}) custom-call(s32[16]{0:T(128)} %tiles_hbm.3, f32[1]{0:T(128)} %bitcast.energy_ref, f32[32,2,8,128]{3,2,1,0:T(8,128)S(1)} %exchange.1.sigma_ref, f32[2,2,128,128]{3,2,1,0:T(8,128)S(1)} %bitcast.8, f32[1,2,128,128]{3,2,1,0:T(8,128)S(1)} %bitcast.10, f32[2,2,128,128]{3,2,1,0:T(8,128)S(1)} %bitcast.9), custom_call_target="tpu_custom_call" | custom-call | tf_op jit(solution)/shard_map/sweep/pallas_call | solution.py:647
Async XLA Ops:
  0.6 23.3 %copy-start = (f32[1,2,2,128,128]{4,3,2,1,0:T(8,128)S(1)}, f32[1,2,2,128,128]{4,3,2,1,0:T(8,128)}, u32[]{:S(2)}) copy-start(f32[1,2,2,128,128]{4,3,2,1,0:T(8,128)} %param.9) | copy-start | bytes 786436
  0.6 23.3 %copy-start.1 = (f32[1,1,2,2,128,128]{5,4,3,2,1,0:T(8,128)S(1)}, f32[1,1,2,2,128,128]{5,4,3,2,1,0:T(8,128)}, u32[]{:S(2)}) copy-start(f32[1,1,2,2,128,128]{5,4,3,2,1,0:T(8,128)} %param.11) | copy-start | bytes 786436
  0.7 23.3 %copy-start.2 = (f32[1,1,2,128,128]{4,3,2,1,0:T(8,128)S(1)}, f32[1,1,2,128,128]{4,3,2,1,0:T(8,128)}, u32[]{:S(2)}) copy-start(f32[1,1,2,128,128]{4,3,2,1,0:T(8,128)} %param.10) | copy-start | bytes 393220

commit v3 on v2

--- a/solution.py
+++ b/solution.py
@@ -284,12 +284,26 @@
 HBM = pl.BlockSpec(memory_space=pltpu.HBM)
 
 
-def half_swap(rows):
-    return pltpu.roll(rows, 4, rows.ndim - 2)
-
-
-def upper_half(shape):
-    return lax.broadcasted_iota(jnp.int32, shape, len(shape) - 2) % 8 < 4
+def rolled(rows, shift):
+    return pltpu.roll(rows, shift, rows.ndim - 2)
+
+
+def sublane(shape):
+    return lax.broadcasted_iota(jnp.int32, shape, len(shape) - 2) % 8
+
+
+def crossed_rows(four):
+    row = sublane(four[0].shape)
+    top, first = row < 4, row % 4 < 2
+    a, b, c, d = four
+    out = []
+    for left, right in (
+        (jnp.where(top, a, rolled(c, 4)), jnp.where(top, b, rolled(d, 4))),
+        (jnp.where(top, rolled(a, 4), c), jnp.where(top, rolled(b, 4), d)),
+    ):
+        out.append(jnp.where(first, left, rolled(right, 2)))
+        out.append(jnp.where(first, rolled(left, 6), right))
+    return out
 
 
 def tile_place(tiles_ref, slot):
@@ -387,95 +401,125 @@
     for k, e in others:
         pl.semaphore_signal(barrier, inc=1, device_id={"ka": k, "ea": e}, device_id_type=MESH)
 
-    top = upper_half((16, 8, 128))
-
-    def pack(kind, ref):
-        real = pack_tiles(tiles_ref, lambda blk, row: ref[blk, 0, pl.ds(row, 32), :])
-        imag = pack_tiles(tiles_ref, lambda blk, row: ref[blk, 1, pl.ds(row, 32), :])
-        packed[:16, kind] = jnp.where(top, real, half_swap(imag))
-        packed[16:, kind] = jnp.where(top, half_swap(real), imag)
+    def spread(ref, pieces):
+        for index, piece in enumerate(crossed_rows(pieces)):
+            start = index % 2 * 16
+            ref[index // 2, start : start + 16] = piece
+
+    def pack(ref):
+        return [
+            pack_tiles(tiles_ref, lambda blk, row: ref[blk, part, pl.ds(row, 32), :])
+            for part in range(2)
+        ]
 
     loads[0].wait()
     loads[1].wait()
     for blk in range(2):
         for part in range(2):
             gt_ref[blk, part] = g_ref[blk, part].T
-    pack(1, gt_ref)
+    greater_rows = pack(gt_ref)
     loads[2].wait()
-    pack(0, l_ref)
+    spread(packed, pack(l_ref) + greater_rows)
     pl.semaphore_wait(barrier, count - 1)
-    for k, e in others:
-        other = k * n_e + e
-        remote(packed.at[other], held.at[me], send_a, recv_a, k, e).start()
-
-    held[me] = packed[me]
+    for chunk in range(2):
+        for k, e in others:
+            source = packed.at[chunk, k * n_e + e]
+            target = held.at[chunk, me]
+            remote(source, target, send_a.at[chunk], recv_a.at[chunk], k, e).start()
+
+    held[0, me] = packed[0, me]
+    held[1, me] = packed[1, me]
     loads[3].wait()
     for blk in range(2):
         ct_ref[blk] = c_ref[blk].T
     for kind, ref in ((0, c_ref), (1, ct_ref)):
         bare = pack_tiles(tiles_ref, lambda blk, row: ref[blk, pl.ds(row, 32), :])
-        bare = bare * bare
-        weight_ref[:16, kind] = jnp.where(top, bare, half_swap(bare))
-        weight_ref[16:, kind] = jnp.where(top, half_swap(bare), bare)
-    scale = SIGMA_SCALE / (n_e * n_k)
-    weight_l = weight_ref[me, 0] * scale
-    weight_g = weight_ref[me, 1] * scale
+        spread(weight_ref.at[kind], [bare * bare * (SIGMA_SCALE / (n_e * n_k))] * 4)
 
     lags = 2 * n_e - 1
-
-    def correlate(k_index, sums):
-        first = k_index * n_e
-        plain, crossed = list(sums[0]), list(sums[1])
-        lesser = [held[first + e, 0] for e in range(n_e)]
-        greater = [held[first + e, 1] for e in range(n_e)]
-        for e_two in range(n_e):
-            swapped = half_swap(greater[e_two])
-            for e_one in range(n_e):
-                lag = e_one - e_two + n_e - 1
-                plain[lag] = plain[lag] + lesser[e_one] * greater[e_two]
-                crossed[lag] = crossed[lag] + lesser[e_one] * swapped
-        return tuple(plain), tuple(crossed)
-
-    all_of(held, send_a, recv_a).wait_recv()
-    zero = jnp.zeros((8, 128), jnp.float32)
-    plain, crossed = lax.fori_loop(0, n_k, correlate, ((zero,) * lags, (zero,) * lags))
-    sign = jnp.where(upper_half((8, 128)), 1.0, -1.0)
-    real = [sign * (total - half_swap(total)) for total in plain]
-    imag = [-sign * (total + half_swap(total)) for total in crossed]
-
-    def convolve(turn, carry):
-        k_index = (my_k + turn) % n_k
-        first = k_index * n_e
-        for kind, weight in ((0, weight_l), (1, weight_g)):
-            green = [held[first + e, kind] for e in range(n_e)]
-            swapped = [half_swap(piece) for piece in green]
-            for e_out in range(n_e):
-                total = None
-                for e_in in range(n_e):
-                    lag = e_out - e_in if kind == 0 else e_in - e_out
-                    lag = lag + n_e - 1
-                    term = green[e_in] * real[lag] + swapped[e_in] * imag[lag]
-                    total = term if total is None else total + term
-                sigma[first + e_out, kind] = total * weight
-
-        def send(e):
-            source = sigma.at[first + e]
-            remote(source, back.at[me], send_b, recv_b, k_index, e).start()
-
-        for e in far + near[1:]:
-            send(e)
-
-        @pl.when(turn > 0)
-        def _():
-            send(my_e)
-
+    row = sublane((8, 128))
+    top, first_pair = row < 4, row % 4 < 2
+    sign = jnp.where(first_pair, 1.0, -1.0)
+
+    def swap(rows):
+        return jnp.where(first_pair, rolled(rows, 6), rolled(rows, 2))
+
+    def greens(chunk, pair):
+        both = []
+        for e in range(n_e):
+            one = held[chunk, 2 * pair * n_e + e]
+            two = held[chunk, (2 * pair + 1) * n_e + e]
+            lesser = jnp.where(top, one, rolled(two, 4))
+            both.append((lesser, jnp.where(top, rolled(one, 4), two)))
+        return [piece[0] for piece in both], [piece[1] for piece in both]
+
+    def work(chunk, carry):
+        all_of(held.at[chunk], send_a.at[chunk], recv_a.at[chunk]).wait_recv()
+
+        def correlate(pair, sums):
+            plain, crossed = list(sums[0]), list(sums[1])
+            lesser, greater = greens(chunk, pair)
+            for e_two in range(n_e):
+                swapped = swap(greater[e_two])
+                for e_one in range(n_e):
+                    lag = e_one - e_two + n_e - 1
+                    plain[lag] = plain[lag] + lesser[e_one] * greater[e_two]
+                    crossed[lag] = crossed[lag] + lesser[e_one] * swapped
+            return tuple(plain), tuple(crossed)
+
+        zero = jnp.zeros((8, 128), jnp.float32)
+        plain, crossed = lax.fori_loop(
+            0, n_k // 2, correlate, ((zero,) * lags, (zero,) * lags)
+        )
+        plain = [total + rolled(total, 4) for total in plain]
+        crossed = [total + rolled(total, 4) for total in crossed]
+        real = [sign * (total - rolled(total, 2)) for total in plain]
+        imag = [-sign * (total + rolled(total, 2)) for total in crossed]
+        weights = weight_ref[0, chunk, me], weight_ref[1, chunk, me]
+
+        def convolve(turn, inner):
+            pair = (my_k // 2 + turn) % (n_k // 2)
+            results = []
+            for kind, green in enumerate(greens(chunk, pair)):
+                swapped = [swap(piece) for piece in green]
+                for e_out in range(n_e):
+                    total = None
+                    for e_in in range(n_e):
+                        lag = e_out - e_in if kind == 0 else e_in - e_out
+                        lag = lag + n_e - 1
+                        term = green[e_in] * real[lag] + swapped[e_in] * imag[lag]
+                        total = term if total is None else total + term
+                    results.append(total * weights[kind])
+            for e in range(n_e):
+                less, more = results[e], results[n_e + e]
+                sigma[chunk, 2 * pair * n_e + e] = jnp.where(top, less, rolled(more, 4))
+                sigma[chunk, (2 * pair + 1) * n_e + e] = jnp.where(top, rolled(less, 4), more)
+
+            def send(k, e):
+                source = sigma.at[chunk, k * n_e + e]
+                target = back.at[chunk, me]
+                remote(source, target, send_b.at[chunk], recv_b.at[chunk], k, e).start()
+
+            for e in far + near[1:]:
+                for k in (2 * pair, 2 * pair + 1):
+                    send(k, e)
+            for k in (2 * pair, 2 * pair + 1):
+
+                @pl.when(k != my_k)
+                def _():
+                    send(k, my_e)
+
+            return inner
+
+        lax.fori_loop(0, n_k // 2, convolve, 0)
+        back[chunk, me] = sigma[chunk, me]
         return carry
 
-    lax.fori_loop(0, n_k, convolve, 0)
-    back[me] = sigma[me]
-    all_of(held, send_a, recv_a).wait_send()
-    all_of(back, send_b, recv_b).wait_send()
-    all_of(back, send_b, recv_b).wait_recv()
+    lax.fori_loop(0, 2, work, 0)
+    for chunk in range(2):
+        all_of(held.at[chunk], send_a.at[chunk], recv_a.at[chunk]).wait_send()
+        all_of(back.at[chunk], send_b.at[chunk], recv_b.at[chunk]).wait_send()
+        all_of(back.at[chunk], send_b.at[chunk], recv_b.at[chunk]).wait_recv()
     out_ref[...] = back[...]
 
 
@@ -543,17 +587,14 @@
 ):
     load = pltpu.make_async_copy(tiles_hbm, tiles_ref, load_sem)
     load.start()
-    top = upper_half((16, 8, 128))
     group = lax.broadcasted_iota(jnp.int32, (32, 128), 1) // 32
     pieces = []
+    parts = crossed_rows(
+        [sigma_ref[index // 2, index % 2 * 16 : index % 2 * 16 + 16] for index in range(4)]
+    )
     for kind in range(2):
-        first, second = sigma_ref[:16, kind], sigma_ref[16:, kind]
-        parts = (
-            jnp.where(top, first, half_swap(second)),
-            jnp.where(top, half_swap(first), second),
-        )
         for part in range(2):
-            packed = parts[part].reshape(128, 128)
+            packed = parts[2 * kind + part].reshape(128, 128)
             pieces.append((kind, part, packed[64:]))
             for blk in range(2):
                 for pos in range(4):
@@ -626,7 +667,7 @@
     count = n_k * n_e
     f32 = jnp.float32
     limit = pltpu.CompilerParams(vmem_limit_bytes=32 * 1024 * 1024)
-    slots = (count, 2, 8, 128)
+    slots = (2, count, 8, 128)
     blocks = pltpu.VMEM((2, 2, 128, 128), f32)
     plane = pltpu.VMEM((2, 128, 128), f32)
     sigma = pl.pallas_call(
@@ -635,9 +676,10 @@
         in_specs=[HBM] * 4,
         out_specs=VMEM,
         scratch_shapes=[pltpu.SMEM((16,), jnp.int32), blocks, blocks, plane, blocks, plane]
-        + [pltpu.VMEM(slots, f32)] * 5
+        + [pltpu.VMEM(slots, f32), pltpu.VMEM((2,) + slots, f32)]
+        + [pltpu.VMEM(slots, f32)] * 3
         + [pltpu.SemaphoreType.DMA((4,))]
-        + [pltpu.SemaphoreType.DMA] * 4,
+        + [pltpu.SemaphoreType.DMA((2,))] * 4,
         compiler_params=pltpu.CompilerParams(
             collective_id=0, has_side_effects=True, vmem_limit_bytes=32 * 1024 * 1024
         ),

time: 29.1 us -> 28.8 us (0.990)
  Pallas kernels: 28.3 us -> 27.9 us
    pallas_call x1, Pallas kernels: 23.2 us -> 22.9 us  [small_device(): pl.pallas_call(partial(exchange_kernel, n_k, n_e), out_shape=jax.ShapeDty...]
where the time goes in v3:
time: 28.8 us; the launch traced here: 28.7 us
  Pallas kernels  27.9 us (97%)
  between operations  0.7 us (2%)
    pallas_call x1, Pallas kernels, small_device(): pl.pallas_call(partial(exchange_kernel, n_k, n_e), out_shape=jax.ShapeDty...  22.9 us
    pallas_call x1, Pallas kernels, small_device(): pl.pallas_call(sweep_kernel, out_shape=(jax.ShapeDtypeStruct((2, 2, 128,...  5.06 us

profile of v3, /device:TPU:0, one launch (start us, length us, event | category | flops | bytes accessed | tf_op | source)
XLA Modules:
  0.0 28.7 jit_solution(5365950900547060885)
XLA Ops:
  0.6 0.0 copy-start
  0.6 0.0 copy-start.1
  0.7 0.0 copy-start.2
  0.7 22.9 %exchange.1.sigma_ref = f32[2,32,8,128]{3,2,1,0:T(8,128)S(1)} custom-call(s32[16]{0:T(128)} %tiles_hbm.3, f32[2,2,128,128]{3,2,1,0:T(8,128)} %bitcast.11, f32[2,2,128,128]{3,2,1,0:T(8,128)} %bitcast.12, f32[2,128,128]{2,1,0:T(8,128)} %c_hbm.1), custom_call_target="tpu_custom_call" | custom-call | tf_op jit(solution)/shard_map/exchange/pallas_call | solution.py:673
  23.6 0.0 copy-done
  23.6 0.0 copy-done.1
  23.6 0.0 copy-done.2
  23.6 5.1 %sweep.1 = (f32[2,2,128,128]{3,2,1,0:T(8,128)}, f32[2,2,128,128]{3,2,1,0:T(8,128)}) custom-call(s32[16]{0:T(128)} %tiles_hbm.3, f32[1]{0:T(128)} %bitcast.energy_ref, f32[2,32,8,128]{3,2,1,0:T(8,128)S(1)} %exchange.1.sigma_ref, f32[2,2,128,128]{3,2,1,0:T(8,128)S(1)} %bitcast.8, f32[1,2,128,128]{3,2,1,0:T(8,128)S(1)} %bitcast.10, f32[2,2,128,128]{3,2,1,0:T(8,128)S(1)} %bitcast.9), custom_call_target="tpu_custom_call" | custom-call | tf_op jit(solution)/shard_map/sweep/pallas_call | solution.py:689
Async XLA Ops:
  0.6 22.9 %copy-start = (f32[1,2,2,128,128]{4,3,2,1,0:T(8,128)S(1)}, f32[1,2,2,128,128]{4,3,2,1,0:T(8,128)}, u32[]{:S(2)}) copy-start(f32[1,2,2,128,128]{4,3,2,1,0:T(8,128)} %param.9) | copy-start | bytes 786436
  0.6 22.9 %copy-start.1 = (f32[1,1,2,2,128,128]{5,4,3,2,1,0:T(8,128)S(1)}, f32[1,1,2,2,128,128]{5,4,3,2,1,0:T(8,128)}, u32[]{:S(2)}) copy-start(f32[1,1,2,2,128,128]{5,4,3,2,1,0:T(8,128)} %param.11) | copy-start | bytes 786436
  0.7 22.9 %copy-start.2 = (f32[1,1,2,128,128]{4,3,2,1,0:T(8,128)S(1)}, f32[1,1,2,128,128]{4,3,2,1,0:T(8,128)}, u32[]{:S(2)}) copy-start(f32[1,1,2,128,128]{4,3,2,1,0:T(8,128)} %param.10) | copy-start | bytes 393220

commit v4 on v3

--- a/solution.py
+++ b/solution.py
@@ -548,7 +548,7 @@
     return jnp.concatenate([rows[:, :128].T, -rows[:, 128:].T], axis=1)
 
 
-def invert_rows(system, eye):
+def first_step(system, eye):
     real_m, imag_m = system[:, :128], system[:, 128:]
     only_re = jnp.where(eye, real_m, 0.0)
     only_im = jnp.where(eye, imag_m, 0.0)
@@ -564,12 +564,9 @@
     twice = jnp.where(eye, 2.0, 0.0)
     inner_re = twice - (real_m * row_re - imag_m * row_im)
     inner_im = -(real_m * row_im + imag_m * row_re)
-    approx = jnp.concatenate(
+    return jnp.concatenate(
         [col_re * inner_re - col_im * inner_im, col_re * inner_im + col_im * inner_re], axis=1
     )
-    product = times(split(system), square_form(approx))
-    rest = jnp.concatenate([twice - product[:, :128], -product[:, 128:]], axis=1)
-    return times(split(approx), square_form(rest))
 
 
 def sweep_kernel(
@@ -628,31 +625,44 @@
         system = shift - rows_of(h_ref, blk) - 0.5 * (more - less)
         return system, less + rows_of(contact_ref, blk)
 
+    twice = jnp.concatenate([jnp.where(eye, 2.0, 0.0), jnp.zeros((128, 128), jnp.float32)], axis=1)
     link = rows_of(link_ref, 0)
     link_square = square_form(link)
     link_adjoint = split(adjoint(link))
 
     system_0, source_0 = system_source(0)
     system_1, source_1 = system_source(1)
-    gr_0 = invert_rows(system_0, eye)
-    gr_0_rows, gr_0_square = split(gr_0), square_form(gr_0)
-    right_op = times(gr_0_rows, link_square)
-    right_square = square_form(right_op)
-    system_1 = system_1 - times(link_adjoint, right_square)
-    gr_1 = invert_rows(system_1, eye)
-    gl_0 = times(split(times(gr_0_rows, square_form(source_0))), gr_0_square, 1)
-    left_l = times(link_adjoint, square_form(gl_0))
-    source_1 = source_1 + times(split(left_l), link_square)
+    x_0 = first_step(system_0, eye)
+    x_0_square = square_form(x_0)
+    product = times(split(system_0), x_0_square)
+    left_x = split(times(link_adjoint, x_0_square))
+    x_0 = split(x_0)
+    through = square_form(2.0 * link - times(split(product), link_square))
+    system_1 = system_1 - times(left_x, through)
+    rest = square_form(twice - product)
+    left_r = times(left_x, rest)
+    gr_0 = times(x_0, rest)
+    right_op = split(times(x_0, through))
+    x_1 = first_step(system_1, eye)
+    product = times(split(system_1), square_form(x_1))
+    source_0_square = square_form(source_0)
+    left_s = split(times(split(left_r), source_0_square))
+    left_r = square_form(left_r)
+    source_1 = square_form(source_1 + times(left_s, left_r, 1))
+    gr_1 = times(split(x_1), square_form(twice - product))
+    gr_0_square = square_form(gr_0)
+    left_l = square_form(times(left_s, gr_0_square, 1))
+    gl_0 = times(split(times(split(gr_0), source_0_square)), gr_0_square, 1)
     gr_1_square = square_form(gr_1)
-    gl_1 = times(split(times(split(gr_1), square_form(source_1))), gr_1_square, 1)
-    left_r = times(link_adjoint, gr_0_square)
-    right_rows = split(right_op)
-    middle = split(times(right_rows, gr_1_square))
-    full_r = gr_0 + times(middle, square_form(left_r))
-    cross = times(middle, square_form(left_l))
-    inner = times(split(times(right_rows, square_form(gl_1))), right_square, 1)
+    middle = times(right_op, gr_1_square)
+    middle_rows = split(middle)
+    carried = times(middle_rows, source_1)
+    cross = times(middle_rows, left_l)
+    gl_1 = times(split(times(split(gr_1), source_1)), gr_1_square, 1)
+    inner = times(split(carried), square_form(middle), 1)
+    full_r = gr_0 + times(middle_rows, left_r)
     full_l = gl_0 + inner - cross - adjoint(cross)
-    for blk, retarded, lesser in ((0, full_r, full_l), (1, gr_1, gl_1)):
+    for blk, retarded, lesser in ((1, gr_1, gl_1), (0, full_r, full_l)):
         greater = lesser + retarded - adjoint(retarded)
         for part in range(2):
             lesser_ref[blk, part] = lesser[:, 128 * part : 128 * part + 128]

time: 28.8 us -> 27.8 us (0.965)
  Pallas kernels: 27.9 us -> 27 us
    pallas_call x1, Pallas kernels: 5.06 us -> 4.07 us  [small_device(): pl.pallas_call(sweep_kernel, out_shape=(jax.ShapeDtypeStruct((2, 2, 128,...]
where the time goes in v4:
time: 27.8 us; the launch traced here: 27.7 us
  Pallas kernels  27 us (97%)
  between operations  0.7 us (3%)
    pallas_call x1, Pallas kernels, small_device(): pl.pallas_call(partial(exchange_kernel, n_k, n_e), out_shape=jax.ShapeDty...  22.9 us
    pallas_call x1, Pallas kernels, small_device(): pl.pallas_call(sweep_kernel, out_shape=(jax.ShapeDtypeStruct((2, 2, 128,...  4.07 us

profile of v4, /device:TPU:0, one launch (start us, length us, event | category | flops | bytes accessed | tf_op | source)
XLA Modules:
  0.0 27.7 jit_solution(3923172660051345993)
XLA Ops:
  0.6 0.0 copy-start
  0.6 0.0 copy-start.1
  0.7 0.0 copy-start.2
  0.7 22.9 %exchange.1.sigma_ref = f32[2,32,8,128]{3,2,1,0:T(8,128)S(1)} custom-call(s32[16]{0:T(128)} %tiles_hbm.3, f32[2,2,128,128]{3,2,1,0:T(8,128)} %bitcast.11, f32[2,2,128,128]{3,2,1,0:T(8,128)} %bitcast.12, f32[2,128,128]{2,1,0:T(8,128)} %c_hbm.1), custom_call_target="tpu_custom_call" | custom-call | tf_op jit(solution)/shard_map/exchange/pallas_call | solution.py:683
  23.6 0.0 copy-done
  23.6 0.0 copy-done.1
  23.6 0.0 copy-done.2
  23.6 4.1 %sweep.1 = (f32[2,2,128,128]{3,2,1,0:T(8,128)}, f32[2,2,128,128]{3,2,1,0:T(8,128)}) custom-call(s32[16]{0:T(128)} %tiles_hbm.3, f32[1]{0:T(128)} %bitcast.energy_ref, f32[2,32,8,128]{3,2,1,0:T(8,128)S(1)} %exchange.1.sigma_ref, f32[2,2,128,128]{3,2,1,0:T(8,128)S(1)} %bitcast.8, f32[1,2,128,128]{3,2,1,0:T(8,128)S(1)} %bitcast.10, f32[2,2,128,128]{3,2,1,0:T(8,128)S(1)} %bitcast.9), custom_call_target="tpu_custom_call" | custom-call | tf_op jit(solution)/shard_map/sweep/pallas_call | solution.py:699
Async XLA Ops:
  0.6 22.9 %copy-start = (f32[1,2,2,128,128]{4,3,2,1,0:T(8,128)S(1)}, f32[1,2,2,128,128]{4,3,2,1,0:T(8,128)}, u32[]{:S(2)}) copy-start(f32[1,2,2,128,128]{4,3,2,1,0:T(8,128)} %param.9) | copy-start | bytes 786436
  0.6 22.9 %copy-start.1 = (f32[1,1,2,2,128,128]{5,4,3,2,1,0:T(8,128)S(1)}, f32[1,1,2,2,128,128]{5,4,3,2,1,0:T(8,128)}, u32[]{:S(2)}) copy-start(f32[1,1,2,2,128,128]{5,4,3,2,1,0:T(8,128)} %param.11) | copy-start | bytes 786436
  0.7 22.9 %copy-start.2 = (f32[1,1,2,128,128]{4,3,2,1,0:T(8,128)S(1)}, f32[1,1,2,128,128]{4,3,2,1,0:T(8,128)}, u32[]{:S(2)}) copy-start(f32[1,1,2,128,128]{4,3,2,1,0:T(8,128)} %param.10) | copy-start | bytes 393220

commit v5 on v4

--- a/solution.py
+++ b/solution.py
@@ -548,25 +548,23 @@
     return jnp.concatenate([rows[:, :128].T, -rows[:, 128:].T], axis=1)
 
 
-def first_step(system, eye):
-    real_m, imag_m = system[:, :128], system[:, 128:]
-    only_re = jnp.where(eye, real_m, 0.0)
-    only_im = jnp.where(eye, imag_m, 0.0)
-
-    def reciprocal(axis):
+def scaled(rows, factor):
+    real, imag = rows[:, :128], rows[:, 128:]
+    return jnp.concatenate(
+        [real * factor[0] - imag * factor[1], real * factor[1] + imag * factor[0]], axis=1
+    )
+
+
+def diagonal_inverse(system, eye):
+    only_re = jnp.where(eye, system[:, :128], 0.0)
+    only_im = jnp.where(eye, system[:, 128:], 0.0)
+    pair = []
+    for axis in range(2):
         real_d = jnp.sum(only_re, axis=axis, keepdims=True)
         imag_d = jnp.sum(only_im, axis=axis, keepdims=True)
         denominator = real_d * real_d + imag_d * imag_d
-        return real_d / denominator, -imag_d / denominator
-
-    row_re, row_im = reciprocal(0)
-    col_re, col_im = reciprocal(1)
-    twice = jnp.where(eye, 2.0, 0.0)
-    inner_re = twice - (real_m * row_re - imag_m * row_im)
-    inner_im = -(real_m * row_im + imag_m * row_re)
-    return jnp.concatenate(
-        [col_re * inner_re - col_im * inner_im, col_re * inner_im + col_im * inner_re], axis=1
-    )
+        pair.append((real_d / denominator, -imag_d / denominator))
+    return pair
 
 
 def sweep_kernel(
@@ -628,33 +626,40 @@
     twice = jnp.concatenate([jnp.where(eye, 2.0, 0.0), jnp.zeros((128, 128), jnp.float32)], axis=1)
     link = rows_of(link_ref, 0)
     link_square = square_form(link)
-    link_adjoint = split(adjoint(link))
 
     system_0, source_0 = system_source(0)
     system_1, source_1 = system_source(1)
-    x_0 = first_step(system_0, eye)
-    x_0_square = square_form(x_0)
-    product = times(split(system_0), x_0_square)
-    left_x = split(times(link_adjoint, x_0_square))
-    x_0 = split(x_0)
-    through = square_form(2.0 * link - times(split(product), link_square))
-    system_1 = system_1 - times(left_x, through)
-    rest = square_form(twice - product)
-    left_r = times(left_x, rest)
-    gr_0 = times(x_0, rest)
-    right_op = split(times(x_0, through))
-    x_1 = first_step(system_1, eye)
-    product = times(split(system_1), square_form(x_1))
+    system_0_square = square_form(system_0)
+    row_0, col_0 = diagonal_inverse(system_0, eye)
+    x_0 = scaled(twice - scaled(system_0, row_0), col_0)
+    link_d = scaled(adjoint(link), row_0)
+    left_u = 2.0 * link_d - scaled(times(split(link_d), system_0_square), row_0)
+    left_rows = split(left_u)
+    left_m = split(times(left_rows, system_0_square))
+    x_0_rows, x_0_square = split(x_0), square_form(x_0)
+    x_link = square_form(times(x_0_rows, link_square))
+    system_1 = system_1 - (2.0 * times(left_rows, link_square) - times(left_m, x_link))
+    system_1_square = square_form(system_1)
+    row_1, col_1 = diagonal_inverse(system_1, eye)
+    x_1 = scaled(twice - scaled(system_1, row_1), col_1)
+    rest = split(twice - times(x_0_rows, system_0_square))
+    right_op = split(times(rest, x_link))
+    x_1_rows, x_1_square = split(x_1), square_form(x_1)
+    right_x = times(right_op, x_1_square)
+    right_m = times(split(right_x), system_1_square)
+    product = times(x_1_rows, system_1_square)
+    gr_0 = times(rest, x_0_square)
+    left_r = 2.0 * left_u - times(left_m, x_0_square)
     source_0_square = square_form(source_0)
     left_s = split(times(split(left_r), source_0_square))
     left_r = square_form(left_r)
     source_1 = square_form(source_1 + times(left_s, left_r, 1))
-    gr_1 = times(split(x_1), square_form(twice - product))
+    middle = 2.0 * right_x - times(split(right_m), x_1_square)
+    gr_1 = times(split(twice - product), x_1_square)
     gr_0_square = square_form(gr_0)
     left_l = square_form(times(left_s, gr_0_square, 1))
     gl_0 = times(split(times(split(gr_0), source_0_square)), gr_0_square, 1)
     gr_1_square = square_form(gr_1)
-    middle = times(right_op, gr_1_square)
     middle_rows = split(middle)
     carried = times(middle_rows, source_1)
     cross = times(middle_rows, left_l)

time: 27.8 us -> 28 us (level)
  no operation moved by 1% of the time
where the time goes in v5:
time: 28 us; the launch traced here: 27.8 us
  Pallas kernels  27.1 us (97%)
  between operations  0.7 us (2%)
    pallas_call x1, Pallas kernels, small_device(): pl.pallas_call(partial(exchange_kernel, n_k, n_e), out_shape=jax.ShapeDty...  22.9 us
    pallas_call x1, Pallas kernels, small_device(): pl.pallas_call(sweep_kernel, out_shape=(jax.ShapeDtypeStruct((2, 2, 128,...  4.23 us

profile of v5, /device:TPU:0, one launch (start us, length us, event | category | flops | bytes accessed | tf_op | source)
XLA Modules:
  0.0 27.8 jit_solution(1664276509701684246)
XLA Ops:
  0.6 0.0 copy-start
  0.6 0.0 copy-start.1
  0.7 0.0 copy-start.2
  0.7 22.9 %exchange.1.sigma_ref = f32[2,32,8,128]{3,2,1,0:T(8,128)S(1)} custom-call(s32[16]{0:T(128)} %tiles_hbm.3, f32[2,2,128,128]{3,2,1,0:T(8,128)} %bitcast.11, f32[2,2,128,128]{3,2,1,0:T(8,128)} %bitcast.12, f32[2,128,128]{2,1,0:T(8,128)} %c_hbm.1), custom_call_target="tpu_custom_call" | custom-call | tf_op jit(solution)/shard_map/exchange/pallas_call | solution.py:688
  23.6 0.0 copy-done
  23.6 0.0 copy-done.1
  23.6 0.0 copy-done.2
  23.6 4.2 %sweep.1 = (f32[2,2,128,128]{3,2,1,0:T(8,128)}, f32[2,2,128,128]{3,2,1,0:T(8,128)}) custom-call(s32[16]{0:T(128)} %tiles_hbm.3, f32[1]{0:T(128)} %bitcast.energy_ref, f32[2,32,8,128]{3,2,1,0:T(8,128)S(1)} %exchange.1.sigma_ref, f32[2,2,128,128]{3,2,1,0:T(8,128)S(1)} %bitcast.8, f32[1,2,128,128]{3,2,1,0:T(8,128)S(1)} %bitcast.10, f32[2,2,128,128]{3,2,1,0:T(8,128)S(1)} %bitcast.9), custom_call_target="tpu_custom_call" | custom-call | tf_op jit(solution)/shard_map/sweep/pallas_call | solution.py:704
Async XLA Ops:
  0.6 22.9 %copy-start = (f32[1,2,2,128,128]{4,3,2,1,0:T(8,128)S(1)}, f32[1,2,2,128,128]{4,3,2,1,0:T(8,128)}, u32[]{:S(2)}) copy-start(f32[1,2,2,128,128]{4,3,2,1,0:T(8,128)} %param.9) | copy-start | bytes 786436
  0.6 22.9 %copy-start.1 = (f32[1,1,2,2,128,128]{5,4,3,2,1,0:T(8,128)S(1)}, f32[1,1,2,2,128,128]{5,4,3,2,1,0:T(8,128)}, u32[]{:S(2)}) copy-start(f32[1,1,2,2,128,128]{5,4,3,2,1,0:T(8,128)} %param.11) | copy-start | bytes 786436
  0.7 22.9 %copy-start.2 = (f32[1,1,2,128,128]{4,3,2,1,0:T(8,128)S(1)}, f32[1,1,2,128,128]{4,3,2,1,0:T(8,128)}, u32[]{:S(2)}) copy-start(f32[1,1,2,128,128]{4,3,2,1,0:T(8,128)} %param.10) | copy-start | bytes 393220

commit v6 on v4

--- a/solution.py
+++ b/solution.py
@@ -468,9 +468,9 @@
             return tuple(plain), tuple(crossed)
 
         zero = jnp.zeros((8, 128), jnp.float32)
-        plain, crossed = lax.fori_loop(
-            0, n_k // 2, correlate, ((zero,) * lags, (zero,) * lags)
-        )
+        plain, crossed = (zero,) * lags, (zero,) * lags
+        for pair in range(n_k // 2):
+            plain, crossed = correlate(pair, (plain, crossed))
         plain = [total + rolled(total, 4) for total in plain]
         crossed = [total + rolled(total, 4) for total in crossed]
         real = [sign * (total - rolled(total, 2)) for total in plain]
@@ -517,10 +517,11 @@
 
     lax.fori_loop(0, 2, work, 0)
     for chunk in range(2):
+        all_of(back.at[chunk], send_b.at[chunk], recv_b.at[chunk]).wait_recv()
+        out_ref[chunk] = back[chunk]
+    for chunk in range(2):
         all_of(held.at[chunk], send_a.at[chunk], recv_a.at[chunk]).wait_send()
         all_of(back.at[chunk], send_b.at[chunk], recv_b.at[chunk]).wait_send()
-        all_of(back.at[chunk], send_b.at[chunk], recv_b.at[chunk]).wait_recv()
-    out_ref[...] = back[...]
 
 
 def split(value):
@@ -644,12 +645,12 @@
     gr_0 = times(x_0, rest)
     right_op = split(times(x_0, through))
     x_1 = first_step(system_1, eye)
-    product = times(split(system_1), square_form(x_1))
+    product = times(split(x_1), square_form(system_1))
     source_0_square = square_form(source_0)
     left_s = split(times(split(left_r), source_0_square))
     left_r = square_form(left_r)
     source_1 = square_form(source_1 + times(left_s, left_r, 1))
-    gr_1 = times(split(x_1), square_form(twice - product))
+    gr_1 = times(split(twice - product), square_form(x_1))
     gr_0_square = square_form(gr_0)
     left_l = square_form(times(left_s, gr_0_square, 1))
     gl_0 = times(split(times(split(gr_0), source_0_square)), gr_0_square, 1)

time: 27.8 us -> 27.7 us (level)
  no operation moved by 1% of the time
where the time goes in v6:
time: 27.7 us; the launch traced here: 27.5 us
  Pallas kernels  26.8 us (97%)
  between operations  0.7 us (3%)
    pallas_call x1, Pallas kernels, small_device(): pl.pallas_call(partial(exchange_kernel, n_k, n_e), out_shape=jax.ShapeDty...  22.9 us
    pallas_call x1, Pallas kernels, small_device(): pl.pallas_call(sweep_kernel, out_shape=(jax.ShapeDtypeStruct((2, 2, 128,...  3.97 us

profile of v6, /device:TPU:0, one launch (start us, length us, event | category | flops | bytes accessed | tf_op | source)
XLA Modules:
  0.0 27.5 jit_solution(107721561672039602)
XLA Ops:
  0.6 0.0 copy-start
  0.6 0.0 copy-start.1
  0.7 0.0 copy-start.2
  0.7 22.9 %exchange.1.sigma_ref = f32[2,32,8,128]{3,2,1,0:T(8,128)S(1)} custom-call(s32[16]{0:T(128)} %tiles_hbm.3, f32[2,2,128,128]{3,2,1,0:T(8,128)} %bitcast.11, f32[2,2,128,128]{3,2,1,0:T(8,128)} %bitcast.12, f32[2,128,128]{2,1,0:T(8,128)} %c_hbm.1), custom_call_target="tpu_custom_call" | custom-call | tf_op jit(solution)/shard_map/exchange/pallas_call | solution.py:684
  23.5 0.0 copy-done
  23.5 0.0 copy-done.1
  23.6 0.0 copy-done.2
  23.6 4.0 %sweep.1 = (f32[2,2,128,128]{3,2,1,0:T(8,128)}, f32[2,2,128,128]{3,2,1,0:T(8,128)}) custom-call(s32[16]{0:T(128)} %tiles_hbm.3, f32[1]{0:T(128)} %bitcast.energy_ref, f32[2,32,8,128]{3,2,1,0:T(8,128)S(1)} %exchange.1.sigma_ref, f32[2,2,128,128]{3,2,1,0:T(8,128)S(1)} %bitcast.8, f32[1,2,128,128]{3,2,1,0:T(8,128)S(1)} %bitcast.10, f32[2,2,128,128]{3,2,1,0:T(8,128)S(1)} %bitcast.9), custom_call_target="tpu_custom_call" | custom-call | tf_op jit(solution)/shard_map/sweep/pallas_call | solution.py:700
Async XLA Ops:
  0.6 22.9 %copy-start = (f32[1,2,2,128,128]{4,3,2,1,0:T(8,128)S(1)}, f32[1,2,2,128,128]{4,3,2,1,0:T(8,128)}, u32[]{:S(2)}) copy-start(f32[1,2,2,128,128]{4,3,2,1,0:T(8,128)} %param.9) | copy-start | bytes 786436
  0.6 22.9 %copy-start.1 = (f32[1,1,2,2,128,128]{5,4,3,2,1,0:T(8,128)S(1)}, f32[1,1,2,2,128,128]{5,4,3,2,1,0:T(8,128)}, u32[]{:S(2)}) copy-start(f32[1,1,2,2,128,128]{5,4,3,2,1,0:T(8,128)} %param.11) | copy-start | bytes 786436
  0.7 22.9 %copy-start.2 = (f32[1,1,2,128,128]{4,3,2,1,0:T(8,128)S(1)}, f32[1,1,2,128,128]{4,3,2,1,0:T(8,128)}, u32[]{:S(2)}) copy-start(f32[1,1,2,128,128]{4,3,2,1,0:T(8,128)} %param.10) | copy-start | bytes 393220
